TPU v7x, 256 devices: a whole 4x4x8 slice. The times are simulated.
256 devices in a mesh: ctx: 32 (over z, x), tp: 8 (over y, core).
Axes of the slice: x: 4, y: 4, z: 8, core: 2. Of those that a mesh axis runs over, the one named last changes fastest.
Arguments:
- streams: bfloat16 [4096, 3, 8192], P('ctx', None, 'tp'), may hold values from -6 to 6
- short_filter: float32 [7, 3, 8192], P(None, None, 'tp'), may hold values from -2 to 2
- long_filter: float32 [128, 8192], P(None, 'tp'), may hold values from -1 to 1
- hyena_grad: bfloat16 [4096, 8192], P('ctx', 'tp'), may hold values from -8 to 8
- queries: bfloat16 [4096, 4096], P('ctx', 'tp'), may hold values from -4000 to 4000
- keys: bfloat16 [4096, 4096], P('ctx', 'tp'), may hold values from -4000 to 4000
- values: bfloat16 [4096, 4096], P('ctx', 'tp'), may hold values from -6 to 6
- gain_q: float32 [4096], P('tp'), may hold values from 0.5 to 1.5
- gain_k: float32 [4096], P('tp'), may hold values from 0.5 to 1.5
- attn_grad: bfloat16 [4096, 4096], P('ctx', 'tp'), may hold values from -8 to 8
Outputs:
- hyena_out: bfloat16 [4096, 8192], P('ctx', 'tp')
- grad_streams: bfloat16 [4096, 3, 8192], P('ctx', None, 'tp')
- grad_short: float32 [7, 3, 8192], P(None, None, 'tp')
- grad_long: float32 [128, 8192], P(None, 'tp')
- attn_out: bfloat16 [4096, 4096], P('ctx', 'tp')
- grad_q: bfloat16 [4096, 4096], P('ctx', 'tp')
- grad_k: bfloat16 [4096, 4096], P('ctx', 'tp')
- grad_v: bfloat16 [4096, 4096], P('ctx', 'tp')
- grad_gain_q: float32 [4096], P('tp')
- grad_gain_k: float32 [4096], P('tp')
All inputs are finite; a program needn't handle non-finite values.
Results may differ from a plain program's by a relative error of at most 0.035.
Values may be sent and summed in bfloat16 or wider, within the bound.
No kernel may reach another device: no remote copies, remote signals or barrier semaphores. Data moves between devices by JAX's collectives and lax.ppermute only.
A program may use at most 128 MiB of HBM per device.

v0:
```python
import functools
import math

import jax
import jax.numpy as jnp
import numpy as np
from jax import lax
from jax.experimental import pallas as pl
from jax.experimental.pallas import tpu as pltpu
from jax.sharding import Mesh
from jax.sharding import PartitionSpec as P

HD = 128
EPS = 1e-06
MASKED = -1e30
ROWS = 128
NZ, NX, NY, NC = 8, 4, 4, 2
HALF = 64
F32 = jnp.float32
BF16 = jnp.bfloat16
MIB = 1024 * 1024


def call(kernel, outs, scratch=(), us=1.0, vmem=6, **kw):
    return pl.pallas_call(
        kernel,
        out_shape=outs,
        scratch_shapes=list(scratch),
        compiler_params=pltpu.CompilerParams(vmem_limit_bytes=vmem * MIB),
        cost_estimate=pl.CostEstimate(flops=int(us * 1.1e9), bytes_accessed=0, transcendentals=0),
        **kw,
    )


def shape(dims, dtype):
    return jax.ShapeDtypeStruct(dims, dtype)


VM = pl.BlockSpec(memory_space=pltpu.VMEM)
SM = pl.BlockSpec(memory_space=pltpu.SMEM)


def transform_tables():
    n = np.arange(256)
    k = np.arange(128) + 0.5
    angle = 2.0 * np.pi * np.outer(k, n) / 256.0
    fwd = np.concatenate([np.cos(angle), -np.sin(angle)], 0)
    inv = np.concatenate([np.cos(angle), -np.sin(angle)], 0).T / 128.0
    lag = inv[128 - np.arange(128)]
    pieces = [fwd[:, :128], fwd[:, 128:]]
    for t in (inv[128:], inv[:128], lag):
        pieces += [t[:, :128], t[:, 128:]]
    t32 = np.concatenate(pieces, 0).astype(np.float32)
    hi = t32.astype(jnp.bfloat16)
    lo = (t32 - hi.astype(np.float32)).astype(jnp.bfloat16)
    return np.stack([hi, lo])


def mm(a, b):
    return jnp.dot(a, b, preferred_element_type=F32)


def table_dot(table, at, x):
    rows = 256 if at < 512 else 128
    hi, lo = table[0, at : at + rows], table[1, at : at + rows]
    if x.dtype == BF16:
        return mm(hi, x) + mm(lo, x)
    xh = x.astype(BF16)
    xl = (x - xh.astype(F32)).astype(BF16)
    return mm(hi, xh) + mm(lo, xh) + mm(hi, xl)


def hyena_kernel(
    st, prev, second, following, hg, sf, lf, tab, after,
    out, gs, head, tail, red, done, ext, gm,
):
    done[...] = jnp.zeros((8, 128), F32)
    def taps(s):
        total = None
        for j in range(7):
            term = sf[s, j : j + 1, :] * ext[s, 16 - j : 272 - j, :]
            total = term if total is None else total + term
        return total

    ext[0, 0:16] = prev[256:272].astype(F32)
    ext[0, 16:144] = st[0].astype(F32)
    ext[0, 144:272] = following[0:128].astype(F32)
    for s in (1, 2):
        ext[s, 0:16] = second[16 * s - 16 : 16 * s].astype(F32)
        ext[s, 16:144] = prev[128 * s - 128 : 128 * s].astype(F32)
        ext[s, 144:272] = st[s].astype(F32)
    gates, ones, twos = taps(0), taps(1), taps(2)
    gate, one, two = gates[0:128], ones[128:256], twos[128:256]
    prod = (ones * twos).astype(BF16)
    up = hg[...].astype(F32)
    gf = up * gate
    gf_next = (following[128:256].astype(F32) * gates[128:256]).astype(BF16)
    spec_x = table_dot(tab, 0, prod[0:128]) + table_dot(tab, 256, prod[128:256])
    spec_h = table_dot(tab, 0, lf[...])
    spec_g0 = table_dot(tab, 0, gf)
    spec_g = spec_g0 + table_dot(tab, 256, gf_next)
    xr, xi = spec_x[:128], spec_x[128:]
    hr, hi = spec_h[:128], spec_h[128:]
    filt = table_dot(tab, 512, xr * hr - xi * hi) + table_dot(tab, 640, xr * hi + xi * hr)
    out[...] = (gate * filt).astype(BF16)
    gr, gi = spec_g[:128], spec_g[128:]
    gprod = table_dot(tab, 768, gr * hr + gi * hi) + table_dot(tab, 896, gi * hr - gr * hi)
    ar, ai = spec_g0[:128], spec_g0[128:]
    glong = table_dot(tab, 1024, ar * xr + ai * xi) + table_dot(tab, 1152, ar * xi - ai * xr)
    gm[:, 128:144] = jnp.zeros_like(gm[:, 128:144])
    gm[0, 0:128] = up * filt
    gm[1, 0:128] = gprod * two
    gm[2, 0:128] = gprod * one
    rows = []
    for s in range(3):
        head[s] = gm[s, 0:16].astype(BF16)
        base = 144 if s else 16
        own = gm[s, 0:128]
        total = None
        for j in range(7):
            term = sf[s, j : j + 1, :] * gm[s, j : j + 128, :]
            total = term if total is None else total + term
            rows.append(jnp.sum(own * ext[s, base - j : base + 128 - j, :], axis=0, keepdims=True))
        rows.append(jnp.zeros_like(rows[-1]))
        gs[s] = total.astype(BF16)
        tail[s] = total[112:128]
    rows.append(jnp.zeros((40, rows[-1].shape[1]), F32))
    every = jnp.concatenate([glong] + rows, 0).astype(BF16)
    for part in range(8):
        at, col = (part % 4) * 48, (part // 4) * 128
        red[part % 4, part // 4] = every[at : at + 48, col : col + 128]


def filter_kernel(idx, p0, p1, p3, p2, long_out, short_out, done, every):
    done[...] = jnp.zeros((8, 128), F32)
    my_x = idx[0]
    for d, ref in ((0, p0), (1, p1), (2, p2), (3, p3)):
        at = pl.multiple_of(lax.rem(my_x + NX - d, NX) * 48, 48)
        for z in range(NZ):
            every[pl.ds(at, 48), z * 128 : z * 128 + 128] = ref[z].astype(F32)
    long_out[...] = every[0:128]
    for s in range(3):
        short_out[s] = every[128 + 8 * s : 135 + 8 * s]


def to_lanes(col_q, col_k):
    both = jnp.concatenate([col_q, col_k], 0)
    return jnp.transpose(jnp.broadcast_to(both, (128, 128)))[0:8]


def to_columns(lanes):
    wide = jnp.transpose(jnp.broadcast_to(lanes[0:1], (128, 128)))
    return wide[0:64, 0:1], wide[64:128, 0:1]


def lane_sum(x):
    total = x[:, 0:128]
    for h in range(1, x.shape[1] // 128):
        total = total + x[:, h * 128 : (h + 1) * 128]
    return jnp.sum(total, axis=1, keepdims=True)


def split3(x):
    high = x.astype(BF16).astype(F32)
    mid = (x - high).astype(BF16).astype(F32)
    return high, mid, x - high - mid


def halves_kernel(idx, keys, values, queries, grads, streams, hg, gq, gk, mine, send, to_next, to_prev, to_second, sems):
    core = idx[1]
    here = pl.multiple_of(core * HALF, HALF)
    there = pl.multiple_of((1 - core) * HALF, HALF)
    end = pl.ds(ROWS - 16, 16)
    pairs = [
        (streams.at[1], to_next.at[pl.ds(0, ROWS)]),
        (streams.at[2], to_next.at[pl.ds(ROWS, ROWS)]),
        (streams.at[0, end], to_next.at[pl.ds(2 * ROWS, 16)]),
        (streams.at[0], to_prev.at[pl.ds(0, ROWS)]),
        (hg, to_prev.at[pl.ds(ROWS, ROWS)]),
        (streams.at[1, end], to_second.at[pl.ds(0, 16)]),
        (streams.at[2, end], to_second.at[pl.ds(16, 16)]),
    ]
    for a, ref in enumerate((keys, values, queries, grads)):
        dst = pl.ds(a * HALF, HALF)
        pairs.append((ref.at[pl.ds(there, HALF)], send.at[dst]))
        pairs.append((ref.at[pl.ds(here, HALF)], mine.at[dst]))
    copies = [pltpu.make_async_copy(src, dst, sems.at[i]) for i, (src, dst) in enumerate(pairs)]
    for c in copies:
        c.start()
    both = jnp.concatenate([gq[...], gk[...]], 0)
    parts = list(split3(both)) + [jnp.zeros((10, 512), F32)]
    send[256:272] = jnp.concatenate(parts, 0).astype(BF16)
    for c in copies:
        c.wait()


def own_gains(gn_q, gn_k):
    return jnp.concatenate([gn_q[...], gn_k[...]], 0)


def other_gains(other):
    wide = other[256:272].astype(F32)
    return wide[0:2] + wide[2:4] + wide[4:6]


def square_kernel(mine, other, out):
    sums = []
    for slot in (2, 0):
        at = slice(slot * HALF, slot * HALF + HALF)
        a, b = mine[at].astype(F32), other[at].astype(F32)
        sums.append(lane_sum(a * a + b * b))
    out[...] = to_lanes(sums[0], sums[1])


def pack_kernel(idx, mine, other, gn_q, gn_k, s0, s1, s2, s3, h0, h1, h2, out, rates):
    core = idx[1]
    rate = lax.rsqrt((s0[...] + s1[...] + s2[...] + s3[...]) / (NY * 8 * HD) + EPS)
    rates[...] = rate
    rate_q, rate_k = to_columns(rate)
    for ref, gains, first in ((mine, own_gains(gn_q, gn_k), core * 4), (other, other_gains(other), (1 - core) * 4)):
        for h in range(4):
            cols = slice(h * 128, (h + 1) * 128)
            key, query = ref[0:64, cols].astype(F32), ref[128:192, cols].astype(F32)
            out[first + h, 0:64] = (key * rate_k * gains[1:2, cols]).astype(BF16)
            out[first + h, 64:128] = ref[64:128, cols]
            out[first + h, 128:192] = (query * rate_q * gains[0:1, cols]).astype(BF16)
            out[first + h, 192:256] = ref[192:256, cols]


def keys_kernel(blk, after, out):
    for z in range(NZ):
        out[z * 128 : z * 128 + 128] = blk[z, 0:128]


def stack_kernel(idx, a, c, b, d, red, out, *parts):
    for i, ref in enumerate((a, b, c, d)):
        out[i] = ref[...]
    for d, part in enumerate(parts):
        part[...] = red[lax.rem(idx[0] + d, NX)]


def scatter_sum_kernel(p0, p1, p2, p3, after, out, done):
    done[...] = jnp.zeros((8, 128), F32)
    total = p0[...].astype(F32) + p1[...].astype(F32) + p2[...].astype(F32) + p3[...].astype(F32)
    out[...] = total.astype(BF16)


def pair_sum_kernel(a, b, after, out, done):
    done[...] = jnp.zeros((8, 128), F32)
    out[...] = (a[...].astype(F32) + b[...].astype(F32)).astype(BF16)


def attention_kernel(
    idx, blk, mine, pair,
    keep, gkeep, csend, osend,
    k_all, v_all, q_all, d_all, s_all, w_all,
):
    my_x, core = idx[0], idx[1]
    for d in range(NX):
        xd = lax.rem(my_x + NX - d, NX)
        for ref, cc in ((mine, core), (pair, 1 - core)):
            at = pl.multiple_of(xd * 128 + cc * 64, 64)
            for z in range(NZ):
                k_all[z, pl.ds(at, 64)] = ref[d, z * 128 : z * 128 + 64]
                v_all[z, pl.ds(at, 64)] = ref[d, z * 128 + 64 : z * 128 + 128]
    for z in range(NZ):
        q_all[z * 64 : z * 64 + 64] = blk[z, 128:192]
        d_all[z * 64 : z * 64 + 64] = blk[z, 192:256]
    scale = 1.0 / math.sqrt(HD)
    power = scale * math.log2(math.e)
    base = my_x * 128 + core * 64
    nt = (((1,), (1,)), ((), ()))
    tn = (((0,), (0,)), ((), ()))

    def first(kz):
        return (kz // 2) * 128

    key_row = lax.broadcasted_iota(jnp.int32, (512, 128), 0)
    lane = lax.broadcasted_iota(jnp.int32, (512, 128), 1)
    query_row = (lane // 64) * 512 + base + lane % 64

    row_max = jnp.full((1, 512), MASKED, F32)
    for kz in range(NZ):
        lo = first(kz)
        sc = lax.dot_general(k_all[kz], q_all[lo:512], nt, preferred_element_type=F32)
        diag = jnp.where(key_row + (kz % 2) * 512 <= query_row, sc[:, 0:128], MASKED)
        sc = diag if lo == 384 else jnp.concatenate([diag, sc[:, 128:]], 1)
        s_all[kz, :, lo:512] = sc
        top = jnp.max(sc, axis=0, keepdims=True)
        top = jnp.maximum(row_max[:, lo:], top)
        row_max = top if lo == 0 else jnp.concatenate([row_max[:, :lo], top], 1)
    row_sum = jnp.zeros((1, 512), F32)
    for kz in range(NZ):
        lo = first(kz)
        p = jnp.exp2((s_all[kz, :, lo:512] - row_max[:, lo:]) * power)
        s_all[kz, :, lo:512] = p
        more = row_sum[:, lo:] + jnp.sum(p, axis=0, keepdims=True)
        row_sum = more if lo == 0 else jnp.concatenate([row_sum[:, :lo], more], 1)
    inv = 1.0 / row_sum
    out_t = jnp.zeros((128, 512), F32)
    for kz in range(NZ):
        lo = first(kz)
        w = (s_all[kz, :, lo:512] * inv[:, lo:]).astype(BF16)
        w_all[kz, :, lo:512] = w
        piece = out_t[:, lo:] + lax.dot_general(v_all[kz], w, tn, preferred_element_type=F32)
        out_t = piece if lo == 0 else jnp.concatenate([out_t[:, :lo], piece], 1)
    out_b = jnp.transpose(out_t).astype(BF16)
    spread_col = jnp.sum(out_b.astype(F32) * d_all[...].astype(F32), axis=1, keepdims=True)
    spread = jnp.transpose(jnp.broadcast_to(spread_col, (512, 128)))[0:1]
    grad_qt = jnp.zeros((128, 512), F32)
    gain_k = jnp.zeros((1, 128), F32)
    for kz in range(NZ):
        lo = first(kz)
        w = w_all[kz, :, lo:512]
        dp = lax.dot_general(v_all[kz], d_all[lo:512], nt, preferred_element_type=F32)
        ds = (w.astype(F32) * (dp - spread[:, lo:])).astype(BF16)
        grad_v = mm(w, d_all[lo:512])
        grad_k = mm(ds, q_all[lo:512]) * scale
        piece = grad_qt[:, lo:] + lax.dot_general(k_all[kz], ds, tn, preferred_element_type=F32)
        grad_qt = piece if lo == 0 else jnp.concatenate([grad_qt[:, :lo], piece], 1)
        gain_k = gain_k + jnp.sum(grad_k * k_all[kz].astype(F32), axis=0, keepdims=True)
        for xx in range(NX):
            at = xx * 1024 + kz * 128
            for arr, val in enumerate((grad_k, grad_v)):
                dst = slice(at + arr * 64, at + arr * 64 + 64)
                half0 = val[xx * 128 : xx * 128 + 64]
                half1 = val[xx * 128 + 64 : xx * 128 + 128]
                keep[dst] = jnp.where(core == 0, half0, half1)
                csend[dst] = jnp.where(core == 0, half1, half0).astype(BF16)
    grad_q = jnp.transpose(grad_qt) * scale
    gain_q = jnp.sum(grad_q * q_all[...].astype(F32), axis=0, keepdims=True)
    gains = jnp.concatenate([gain_q, gain_k, jnp.zeros((6, 128), F32)], 0)
    gkeep[...] = gains
    high = gains.astype(BF16).astype(F32)
    csend[4096:4112] = jnp.concatenate([high, gains - high], 0).astype(BF16)
    for z in range(NZ):
        osend[z, 0:64] = out_b[z * 64 : z * 64 + 64]
        osend[z, 64:128] = grad_q[z * 64 : z * 64 + 64].astype(BF16)


def gains_of(rows16):
    wide = rows16.astype(F32)
    return wide[0:8] + wide[8:16]


def core_sum_kernel(idx, keep, gkeep, other, after, s0, g0, s1, s2, s3):
    my_x = idx[0]
    gains = gkeep[...] + gains_of(other[4096:4112])
    g0[...] = gains
    high = gains.astype(BF16).astype(F32)
    rows = jnp.concatenate([high, gains - high], 0).astype(BF16)
    for d, ref in enumerate((s0, s1, s2, s3)):
        at = pl.multiple_of(lax.rem(my_x + d, NX) * 1024, 1024)
        total = keep[pl.ds(at, 1024)] + other[pl.ds(at, 1024)].astype(F32)
        ref[0:1024] = total.astype(ref.dtype)
        if d:
            ref[1024:1040] = rows


def ring_sum_kernel(s0, g0, r1, r2, r3, osend, after, out, done):
    done[...] = g0[...]
    gains = g0[...] + gains_of(r1[1024:1040]) + gains_of(r2[1024:1040]) + gains_of(r3[1024:1040])
    high = gains.astype(BF16).astype(F32)
    rows = jnp.concatenate([high, gains - high], 0).astype(BF16)
    for z in range(NZ):
        at = slice(z * 128, z * 128 + 128)
        total = s0[at] + r1[at].astype(F32) + r2[at].astype(F32) + r3[at].astype(F32)
        out[z, 0:128] = total.astype(BF16)
        out[z, 128:256] = osend[z]
        out[z, 256:272] = rows


def inner_kernel(idx, back, mine, other, gn_q, gn_k, after, part, gains_q, gains_k):
    core = idx[1]
    sum_q = jnp.zeros((64, 128), F32)
    sum_k = jnp.zeros((64, 128), F32)
    for ref, gain, first in ((mine, own_gains(gn_q, gn_k), core * 4), (other, other_gains(other), (1 - core) * 4)):
        for h in range(4):
            cols = slice(h * 128, (h + 1) * 128)
            gk = back[first + h, 0:64].astype(F32)
            gq = back[first + h, 192:256].astype(F32)
            sum_q = sum_q + gq * gain[0:1, cols] * ref[128:192, cols].astype(F32)
            sum_k = sum_k + gk * gain[1:2, cols] * ref[0:64, cols].astype(F32)
    part[...] = to_lanes(
        jnp.sum(sum_q, axis=1, keepdims=True), jnp.sum(sum_k, axis=1, keepdims=True)
    )
    for h in range(4):
        cols = slice(h * 128, (h + 1) * 128)
        got = gains_of(back[core * 4 + h, 256:272])
        gains_q[0:1, cols] = got[0:1] / gn_q[:, cols]
        gains_k[0:1, cols] = got[1:2] / gn_k[:, cols]


def norm_kernel(idx, back, mine, other, gn_q, gn_k, rates, p0, p1, p2, p3, keep, send):
    core = idx[1]
    rate_q, rate_k = to_columns(rates[...])
    inner_q, inner_k = to_columns(p0[...] + p1[...] + p2[...] + p3[...])
    width = NY * 8 * HD
    coef_q = rate_q * rate_q * rate_q * inner_q / width
    coef_k = rate_k * rate_k * rate_k * inner_k / width
    for ref, gain, first, dst in (
        (mine, own_gains(gn_q, gn_k), core * 4, keep), (other, other_gains(other), (1 - core) * 4, send)
    ):
        for h in range(4):
            cols = slice(h * 128, (h + 1) * 128)
            gk = back[first + h, 0:64].astype(F32)
            gq = back[first + h, 192:256].astype(F32)
            raw_k, raw_q = ref[0:64, cols].astype(F32), ref[128:192, cols].astype(F32)
            dst[0, :, cols] = (rate_q * (gq * gain[0:1, cols]) - raw_q * coef_q).astype(BF16)
            dst[1, :, cols] = (rate_k * (gk * gain[1:2, cols]) - raw_k * coef_k).astype(BF16)
            dst[2, :, cols] = back[first + h, 64:128]
            dst[3, :, cols] = back[first + h, 128:192]


def join_kernel(idx, mine, got, q_out, k_out, v_out, o_out):
    core = idx[1]
    here = pl.ds(pl.multiple_of(core * HALF, HALF), HALF)
    there = pl.ds(pl.multiple_of((1 - core) * HALF, HALF), HALF)
    for slot, dst in enumerate((q_out, k_out, v_out, o_out)):
        dst[here, :] = mine[slot]
        dst[there, :] = got[slot]


def rotate(x, axis, size, by):
    return lax.ppermute(x, axis, [(i, (i + by) % size) for i in range(size)])


def flip(x, axis, size, by):
    return lax.ppermute(x, axis, [(i, i ^ by) for i in range(size)])


def along(x, by):
    count = NZ * NX
    return lax.ppermute(
        x, ("z", "x"), [(i, i + by) for i in range(count) if 0 <= i + by < count]
    )


def add16(a, b):
    return (a.astype(F32) + b.astype(F32)).astype(BF16)


def local(
    streams, short_filter, long_filter, hyena_grad, queries, keys, values, gain_q, gain_k, attn_grad
):
    channels = streams.shape[2]
    my_x = lax.axis_index("x")
    core = lax.axis_index("c")
    idx = jnp.stack([my_x, core, lax.axis_index("z")]).astype(jnp.int32)

    gains = (gain_q.reshape(1, 512), gain_k.reshape(1, 512))
    ANY = pl.BlockSpec(memory_space=pl.ANY)
    tab = jnp.asarray(transform_tables())
    st = streams.transpose(1, 0, 2)
    sf = short_filter.transpose(1, 0, 2)
    mine, send, to_next, to_prev, to_second = call(
        halves_kernel,
        [
            shape((256, 512), BF16), shape((272, 512), BF16), shape((272, channels), BF16),
            shape((256, channels), BF16), shape((32, channels), BF16),
        ],
        [pltpu.SemaphoreType.DMA((15,))],
        in_specs=[SM] + [ANY] * 6 + [VM] * 2,
        out_specs=[VM] * 5,
        us=1.0,
        vmem=60,
    )(idx, keys, values, queries, attn_grad, st, hyena_grad, *gains)
    other = rotate(send, "c", NC, 1)
    second = along(to_second, 2)
    prev = along(to_next, 1)
    following = along(to_prev, -1)

    squares = call(square_kernel, shape((8, 128), F32), in_specs=[VM, VM], out_specs=VM, us=0.7)(mine, other)
    sums = [squares] + [rotate(squares, "y", NY, d) for d in (1, 3, 2)]
    payload, rates = call(
        pack_kernel,
        [shape((8, 256, 128), BF16), shape((8, 128), F32)],
        in_specs=[SM] + [VM] * 8 + [ANY] * 3,
        out_specs=[VM, VM],
        us=1.5,
    )(idx, mine, other, *gains, *sums, prev, following, second)
    blk = lax.all_to_all(payload, "z", 0, 0)

    tile = 256
    grid = (channels // tile,)

    def spec(*lead):
        zeros = (0,) * len(lead)
        return pl.BlockSpec(lead + (tile,), lambda i: zeros + (i,))

    def whole(*dims):
        zeros = (0,) * len(dims)
        return pl.BlockSpec(dims, lambda i: zeros)

    hyena_out, gs, head, tail, red, hyena_done = call(
        hyena_kernel,
        [
            shape((ROWS, channels), BF16),
            shape((3, ROWS, channels), BF16),
            shape((3, 16, channels), BF16),
            shape((3, 16, channels), F32),
            shape((NX, NZ, 48, 128), BF16),
            shape((8, 128), F32),
        ],
        [pltpu.VMEM((3, 272, tile), F32), pltpu.VMEM((3, 144, tile), F32)],
        grid=grid,
        in_specs=[
            spec(3, 128), spec(272), spec(32), spec(256), spec(128),
            spec(3, 7), spec(128), whole(2, 1280, 128), ANY,
        ],
        out_specs=[
            spec(128), spec(3, 128), spec(3, 16), spec(3, 16), pl.BlockSpec((NX, 2, 48, 128), lambda i: (0, i, 0, 0)), VM,
        ],
        us=11.0, vmem=56,
    )(st, prev, second, following, hyena_grad, sf, long_filter, tab, rates)
    next_head = along(head, -1)

    kv = call(
        keys_kernel, shape((NZ * 128, HD), BF16), in_specs=[VM, ANY], out_specs=VM, us=0.5
    )(blk, hyena_done)
    piece_shape = shape((NZ, 48, 128), BF16)
    ring, *parts = call(
        stack_kernel,
        [shape((NX, NZ * 128, HD), BF16)] + [piece_shape] * NX,
        in_specs=[SM] + [VM] * 5, out_specs=[VM] * 5, us=1.0,
    )(idx, kv, *[rotate(kv, "x", NX, d) for d in (2, 1, 3)], red)
    parts = parts[:1] + [rotate(parts[d], "x", NX, d) for d in (1, 2, 3)]
    pair = rotate(ring, "c", NC, 1)

    keep, gkeep, csend, osend = call(
        attention_kernel,
        [
            shape((4096, 128), F32), shape((8, 128), F32), shape((4112, 128), BF16),
            shape((8, 128, 128), BF16),
        ],
        [
            pltpu.VMEM((8, 512, 128), BF16), pltpu.VMEM((8, 512, 128), BF16),
            pltpu.VMEM((512, 128), BF16), pltpu.VMEM((512, 128), BF16),
            pltpu.VMEM((8, 512, 512), F32), pltpu.VMEM((8, 512, 512), BF16),
        ],
        in_specs=[SM] + [VM] * 3,
        out_specs=[VM] * 4,
        us=7.0, vmem=28,
    )(idx, blk, ring, pair)
    from_core = rotate(csend, "c", NC, 1)

    token = shape((8, 128), F32)
    piece, scattered = call(
        scatter_sum_kernel, [piece_shape, token], in_specs=[VM] * 4 + [ANY], out_specs=[VM] * 2, us=0.6
    )(*parts, gkeep)
    s0, g0, s1, s2, s3 = call(
        core_sum_kernel,
        [shape((1024, 128), F32), shape((8, 128), F32)] + [shape((1040, 128), BF16)] * 3,
        in_specs=[SM] + [VM] * 3 + [ANY],
        out_specs=[VM] * 5,
        us=1.0,
    )(idx, keep, gkeep, from_core, scattered)
    rest = [rotate(s, "x", NX, d) for d, s in ((1, s1), (3, s3), (2, s2))]
    for by in (1, 4, 2):
        piece, added = call(
            pair_sum_kernel, [piece_shape, token], in_specs=[VM] * 2 + [ANY], out_specs=[VM] * 2, us=0.6
        )(piece, flip(piece, "z", NZ, by), g0)
    outgoing, summed = call(
        ring_sum_kernel,
        [shape((8, 272, 128), BF16), shape((8, 128), F32)],
        in_specs=[VM] * 6 + [ANY], out_specs=[VM] * 2, us=1.0,
    )(s0, g0, *rest, osend, added)
    back = lax.all_to_all(outgoing, "z", 0, 0)

    pieces = [piece] + [rotate(piece, "x", NX, d) for d in (1, 3, 2)]
    grad_long, short_rows, filters = call(
        filter_kernel,
        [shape((128, channels), F32), shape((3, 7, channels), F32), shape((8, 128), F32)],
        in_specs=[SM] + [VM] * 4, out_specs=[VM] * 3, scratch=[pltpu.VMEM((192, channels), F32)],
        us=1.0,
    )(idx, *pieces)
    grad_short = short_rows.transpose(1, 0, 2)
    half_shape = shape((4, HALF, 512), BF16)
    part, gain_grad_q, gain_grad_k = call(
        inner_kernel,
        [shape((8, 128), F32), shape((1, 512), F32), shape((1, 512), F32)],
        in_specs=[SM] + [VM] * 5 + [ANY],
        out_specs=[VM] * 3,
        us=1.0,
    )(idx, back, mine, other, *gains, filters)
    parts = [part] + [rotate(part, "y", NY, d) for d in (1, 3, 2)]
    kept, send = call(
        norm_kernel,
        [half_shape, half_shape],
        in_specs=[SM] + [VM] * 10,
        out_specs=[VM] * 2,
        us=1.0,
    )(idx, back, mine, other, *gains, rates, *parts)
    got = rotate(send, "c", NC, 1)
    grad_q, grad_k, grad_v, attn_out = call(
        join_kernel,
        [shape((ROWS, 512), BF16)] * 4,
        in_specs=[SM] + [VM] * 2,
        out_specs=[VM] * 4,
        us=1.0,
    )(idx, kept, got)

    after = next_head.astype(F32)
    extra = jnp.zeros((3, 16, channels), F32)
    for j in range(1, 7):
        moved = jnp.pad(after[:, 0:j], ((0, 0), (16 - j, 0), (0, 0)))
        extra = extra + sf[:, j : j + 1] * moved
    last = (tail + extra).astype(BF16)
    grad_streams = jnp.concatenate([gs[:, 0:112], last], 1).transpose(1, 0, 2)
    return (
        hyena_out, grad_streams, grad_short, grad_long, attn_out, grad_q, grad_k, grad_v,
        gain_grad_q.reshape(512), gain_grad_k.reshape(512),
    )


def solution(mesh):
    fine = Mesh(mesh.devices.reshape(NZ, NX, NY, NC), ("z", "x", "y", "c"))
    ctx, tp = ("z", "x"), ("y", "c")
    return jax.shard_map(
        local,
        mesh=fine,
        in_specs=(
            P(ctx, None, tp), P(None, None, tp), P(None, tp), P(ctx, tp), P(ctx, tp),
            P(ctx, tp), P(ctx, tp), P(tp), P(tp), P(ctx, tp),
        ),
        out_specs=(
            P(ctx, tp), P(ctx, None, tp), P(None, None, tp), P(None, tp), P(ctx, tp),
            P(ctx, tp), P(ctx, tp), P(ctx, tp), P(tp), P(tp),
        ),
        check_vma=False,
    )
```

profile of v0, /device:TPU:1, one launch (start us, length us, event | category | flops | bytes accessed | tf_op | source)
XLA Modules:
  0.0 147.0 jit_solution(17644644983674534858)
XLA Ops:
  1.2 3.3 %shard_map.186 = (bf16[256,512]{1,0:T(8,128)(2,1)}, bf16[272,512]{1,0:T(8,128)(2,1)}, bf16[272,1024]{1,0:T(8,128)(2,1)}, bf16[256,1024]{1,0:T(8,128)(2,1)}, bf16[32,1024]{1,0:T(8,128)(2,1)}) custom-call(s32[3]{0:T(128)} %pad_add_fusion.idx, bf16[128,512]{1,0:T(8,128)(2,1)} %keys.1, bf16[128,512]{1,0:T(8,128)(2,1)} %values.1, bf16[128,512]{1,0:T(8,128)(2,1)} %queries.1, ...), custom_call_target="tpu_custom_call" | custom-call | flops 1100000000 | tf_op jit(solution)/shard_map/pallas_call | solution.py:456
  4.6 4.1 %collective-permute-start = (bf16[272,1024]{1,0:T(8,128)(2,1)}, bf16[272,1024]{1,0:T(8,128)(2,1)S(1)}, u32[]{:S(2)}, u32[]{:S(2)}) collective-permute-start(bf16[272,1024]{1,0:T(8,128)(2,1)} %get-tuple-element.56), channel_id=1, source_target_pairs={{0,8},{8,16},{16,24},{24,32},{32,40},{40,48},{48,56},{56,64},{64,7... | collective-permute-start | bytes 1671176 | tf_op jit(solution)/shard_map/ppermute | solution.py:434
  11.1 5.8 %collective-permute-start.1 = (bf16[32,1024]{1,0:T(8,128)(2,1)}, bf16[32,1024]{1,0:T(8,128)(2,1)S(1)}, u32[]{:S(2)}, u32[]{:S(2)}) collective-permute-start(bf16[32,1024]{1,0:T(8,128)(2,1)} %get-tuple-element.57), channel_id=1, source_target_pairs={{0,16},{8,24},{16,32},{24,40},{32,48},{40,56},{48,64},{56,72},{64,... | collective-permute-start | bytes 196616 | tf_op jit(solution)/shard_map/ppermute | solution.py:434
  18.0 3.0 %collective-permute-start.6 = (f32[8,128]{1,0:T(8,128)S(1)}, f32[8,128]{1,0:T(8,128)S(1)}, u32[]{:S(2)}, u32[]{:S(2)}) collective-permute-start(f32[8,128]{1,0:T(8,128)S(1)} %shard_map.187.s0), channel_id=1, source_target_pairs={{0,4},{2,6},{4,0},{6,2},{1,5},{3,7},{5,1},{7,3},{8,12},{10,14},{12... | collective-permute-start | bytes 12296 | tf_op jit(solution)/shard_map/ppermute | solution.py:425
  23.8 1.7 %collective-permute-done.4.s1 = f32[8,128]{1,0:T(8,128)S(1)} collective-permute-done((f32[8,128]{1,0:T(8,128)S(1)}, f32[8,128]{1,0:T(8,128)S(1)}, u32[]{:S(2)}, u32[]{:S(2)}) %collective-permute-start.4) | collective-permute-done | bytes 4128 | tf_op jit(solution)/shard_map/ppermute | solution.py:425
  25.5 1.6 %shard_map.188 = (bf16[8,256,128]{2,1,0:T(8,128)(2,1)}, f32[8,128]{1,0:T(8,128)S(1)}) custom-call(s32[3]{0:T(128)S(1)} %copy-done, bf16[256,512]{1,0:T(8,128)(2,1)S(1)} %copy-done.8, bf16[272,512]{1,0:T(8,128)(2,1)S(1)} %collective-permute-done.3.other, f32[1,512]{1,0:T(1,128)S(1)} %bitcast.25, f32[1,512]{1,0:T(1,128)S(1)} %bitcast.29, ...), custom_call_target="tpu_custom_call" | custom-call | flops 1650000000 | tf_op jit(solution)/shard_map/pallas_call | solution.py:475
  27.7 11.9 %all-to-all-start = ((bf16[8,256,128]{2,1,0:T(8,128)(2,1)}), bf16[8,256,128]{2,1,0:T(8,128)(2,1)S(1)}, u32[]{:S(2)}, u32[]{:S(2)}) async-start(bf16[8,256,128]{2,1,0:T(8,128)(2,1)} %get-tuple-element.66), calls=%async_computation | async-start | bytes 1048576 | tf_op jit(solution)/shard_map/all_to_all | solution.py:482
  39.6 11.7 %shard_map.189 = (bf16[128,1024]{1,0:T(8,128)(2,1)}, bf16[3,128,1024]{2,1,0:T(8,128)(2,1)}, bf16[3,16,1024]{2,1,0:T(8,128)(2,1)}, f32[3,16,1024]{2,1,0:T(8,128)}...) custom-call(bf16[3,128,1024]{2,1,0:T(8,128)(2,1)} %bitcast.35, bf16[272,1024]{1,0:T(8,128)(2,1)} %copy-done.1, ...), custom_call_target="tpu_custom_call" | custom-call | flops 12099999744 | tf_op jit(solution)/shard_map/pallas_call | solution.py:495
  51.3 2.9 %all-to-all-done.blk = bf16[8,256,128]{2,1,0:T(8,128)(2,1)S(1)} async-done(((bf16[8,256,128]{2,1,0:T(8,128)(2,1)}), bf16[8,256,128]{2,1,0:T(8,128)(2,1)S(1)}, u32[]{:S(2)}, u32[]{:S(2)}) %all-to-all-start) | async-done | bytes 524320 | tf_op jit(solution)/shard_map/all_to_all | solution.py:482
  54.9 1.4 collective-permute-start.10
  57.6 2.7 %collective-permute-done.10.d = bf16[1024,128]{1,0:T(8,128)(2,1)S(1)} collective-permute-done((bf16[1024,128]{1,0:T(8,128)(2,1)S(1)}, bf16[1024,128]{1,0:T(8,128)(2,1)S(1)}, u32[]{:S(2)}, u32[]{:S(2)}) %collective-permute-start.10) | collective-permute-done | bytes 262176 | tf_op jit(solution)/shard_map/ppermute | solution.py:425
  60.2 5.9 %collective-permute-done.9.b = bf16[1024,128]{1,0:T(8,128)(2,1)S(1)} collective-permute-done((bf16[1024,128]{1,0:T(8,128)(2,1)S(1)}, bf16[1024,128]{1,0:T(8,128)(2,1)S(1)}, u32[]{:S(2)}, u32[]{:S(2)}) %collective-permute-start.9) | collective-permute-done | bytes 262176 | tf_op jit(solution)/shard_map/ppermute | solution.py:425
  66.8 6.0 %collective-permute-start.14 = (bf16[4,1024,128]{2,1,0:T(8,128)(2,1)S(1)}, bf16[4,1024,128]{2,1,0:T(8,128)(2,1)S(1)}, u32[]{:S(2)}, u32[]{:S(2)}) collective-permute-start(bf16[4,1024,128]{2,1,0:T(8,128)(2,1)S(1)} %get-tuple-element.73.mine), channel_id=1, source_target_pairs={{0,1},{1,0},{2,3},{3,2},{4,5},{5,4},{6,7},{7,6},{8,9},{9,8},{10,11... | collective-permute-start | bytes 3145736 | tf_op jit(solution)/shard_map/ppermute | solution.py:425
  72.8 2.3 %collective-permute-done.14.pair = bf16[4,1024,128]{2,1,0:T(8,128)(2,1)S(1)} collective-permute-done((bf16[4,1024,128]{2,1,0:T(8,128)(2,1)S(1)}, bf16[4,1024,128]{2,1,0:T(8,128)(2,1)S(1)}, u32[]{:S(2)}, u32[]{:S(2)}) %collective-permute-start.14) | collective-permute-done | bytes 1048608 | tf_op jit(solution)/shard_map/ppermute | solution.py:425
  75.0 6.1 %shard_map.192 = (f32[4096,128]{1,0:T(8,128)S(1)}, f32[8,128]{1,0:T(8,128)S(1)}, bf16[4112,128]{1,0:T(8,128)(2,1)S(1)}, bf16[8,128,128]{2,1,0:T(8,128)(2,1)S(1)}) custom-call(s32[3]{0:T(128)S(1)} %copy-done, bf16[8,256,128]{2,1,0:T(8,128)(2,1)S(1)} %all-to-all-done.blk, bf16[4,1024,128]{2,1,0:T(8,128)(2,1)S(1)} %get-tuple-element.73.mine, ...), custom_call_target="tpu_custom_call" | custom-call | flops 7699999744 | tf_op jit(solution)/shard_map/pallas_call | solution.py:530
  81.6 1.7 %collective-permute-start.12 = (bf16[8,48,128]{2,1,0:T(8,128)(2,1)S(1)}, bf16[8,48,128]{2,1,0:T(8,128)(2,1)S(1)}, u32[]{:S(2)}, u32[]{:S(2)}) collective-permute-start(bf16[8,48,128]{2,1,0:T(8,128)(2,1)S(1)} %get-tuple-element.71), channel_id=1, source_target_pairs={{0,16},{8,24},{16,0},{24,8},{1,17},{9,25},{17,1},{25,9},{2,18},{10... | collective-permute-start | bytes 294920 | tf_op jit(solution)/shard_map/ppermute | solution.py:425
  84.3 4.9 %collective-permute-done.11.p1 = bf16[8,48,128]{2,1,0:T(8,128)(2,1)S(1)} collective-permute-done((bf16[8,48,128]{2,1,0:T(8,128)(2,1)S(1)}, bf16[8,48,128]{2,1,0:T(8,128)(2,1)S(1)}, u32[]{:S(2)}, u32[]{:S(2)}) %collective-permute-start.11) | collective-permute-done | bytes 98336 | tf_op jit(solution)/shard_map/ppermute | solution.py:425
  90.4 2.7 %collective-permute-done.15.b = bf16[8,48,128]{2,1,0:T(8,128)(2,1)S(1)} collective-permute-done((bf16[8,48,128]{2,1,0:T(8,128)(2,1)S(1)}, bf16[8,48,128]{2,1,0:T(8,128)(2,1)S(1)}, u32[]{:S(2)}, u32[]{:S(2)}) %collective-permute-start.15) | collective-permute-done | bytes 98336 | tf_op jit(solution)/shard_map/ppermute | solution.py:429
  93.7 3.2 %collective-permute-start.17 = (bf16[8,48,128]{2,1,0:T(8,128)(2,1)S(1)}, bf16[8,48,128]{2,1,0:T(8,128)(2,1)S(1)}, u32[]{:S(2)}, u32[]{:S(2)}) collective-permute-start(bf16[8,48,128]{2,1,0:T(8,128)(2,1)S(1)} %get-tuple-element.80.a), channel_id=1, source_target_pairs={{0,128},{32,160},{64,192},{96,224},{128,0},{160,32},{192,64},{224,... | collective-permute-start | bytes 294920 | tf_op jit(solution)/shard_map/ppermute | solution.py:429
  97.2 2.4 %collective-permute-start.23 = (bf16[1040,128]{1,0:T(8,128)(2,1)S(1)}, bf16[1040,128]{1,0:T(8,128)(2,1)S(1)}, u32[]{:S(2)}, u32[]{:S(2)}) collective-permute-start(bf16[1040,128]{1,0:T(8,128)(2,1)S(1)} %get-tuple-element.87), channel_id=1, source_target_pairs={{0,24},{8,0},{16,8},{24,16},{1,25},{9,1},{17,9},{25,17},{2,26},{10... | collective-permute-start | bytes 798728 | tf_op jit(solution)/shard_map/ppermute | solution.py:425
  102.4 4.8 %collective-permute-done.18.b = bf16[8,48,128]{2,1,0:T(8,128)(2,1)S(1)} collective-permute-done((bf16[8,48,128]{2,1,0:T(8,128)(2,1)S(1)}, bf16[8,48,128]{2,1,0:T(8,128)(2,1)S(1)}, u32[]{:S(2)}, u32[]{:S(2)}) %collective-permute-start.18) | collective-permute-done | bytes 98336 | tf_op jit(solution)/shard_map/ppermute | solution.py:429
  107.2 3.4 %collective-permute-done.24.r3 = bf16[1040,128]{1,0:T(8,128)(2,1)S(1)} collective-permute-done((bf16[1040,128]{1,0:T(8,128)(2,1)S(1)}, bf16[1040,128]{1,0:T(8,128)(2,1)S(1)}, u32[]{:S(2)}, u32[]{:S(2)}) %collective-permute-start.24) | collective-permute-done | bytes 266272 | tf_op jit(solution)/shard_map/ppermute | solution.py:425
  111.6 3.5 %all-to-all-start.1 = ((bf16[8,272,128]{2,1,0:T(8,128)(2,1)}), bf16[8,272,128]{2,1,0:T(8,128)(2,1)S(1)}, u32[]{:S(2)}, u32[]{:S(2)}) async-start(bf16[8,272,128]{2,1,0:T(8,128)(2,1)} %get-tuple-element.91), calls=%async_computation.1 | async-start | bytes 1114112 | tf_op jit(solution)/shard_map/all_to_all | solution.py:568
  115.3 3.0 %collective-permute-start.20 = (bf16[8,48,128]{2,1,0:T(8,128)(2,1)S(1)}, bf16[8,48,128]{2,1,0:T(8,128)(2,1)S(1)}, u32[]{:S(2)}, u32[]{:S(2)}) collective-permute-start(bf16[8,48,128]{2,1,0:T(8,128)(2,1)S(1)} %get-tuple-element.82.p0), channel_id=1, source_target_pairs={{0,24},{8,0},{16,8},{24,16},{1,25},{9,1},{17,9},{25,17},{2,26},{10... | collective-permute-start | bytes 294920 | tf_op jit(solution)/shard_map/ppermute | solution.py:425
  120.5 2.5 %collective-permute-done.19.p1 = bf16[8,48,128]{2,1,0:T(8,128)(2,1)S(1)} collective-permute-done((bf16[8,48,128]{2,1,0:T(8,128)(2,1)S(1)}, bf16[8,48,128]{2,1,0:T(8,128)(2,1)S(1)}, u32[]{:S(2)}, u32[]{:S(2)}) %collective-permute-start.19) | collective-permute-done | bytes 98336 | tf_op jit(solution)/shard_map/ppermute | solution.py:425
  123.0 1.5 shard_map.198
  124.4 5.8 %all-to-all-done.1.back = bf16[8,272,128]{2,1,0:T(8,128)(2,1)S(1)} async-done(((bf16[8,272,128]{2,1,0:T(8,128)(2,1)}), bf16[8,272,128]{2,1,0:T(8,128)(2,1)S(1)}, u32[]{:S(2)}, u32[]{:S(2)}) %all-to-all-start.1) | async-done | bytes 557088 | tf_op jit(solution)/shard_map/all_to_all | solution.py:568
  130.2 1.3 shard_map.200
  131.5 2.3 %collective-permute-start.27 = (f32[8,128]{1,0:T(8,128)S(1)}, f32[8,128]{1,0:T(8,128)S(1)}, u32[]{:S(2)}, u32[]{:S(2)}) collective-permute-start(f32[8,128]{1,0:T(8,128)S(1)} %get-tuple-element.93.p0), channel_id=1, source_target_pairs={{0,4},{2,6},{4,0},{6,2},{1,5},{3,7},{5,1},{7,3},{8,12},{10,14},{12... | collective-permute-start | bytes 12296 | tf_op jit(solution)/shard_map/ppermute | solution.py:425
  136.2 2.0 %collective-permute-done.25.p1 = f32[8,128]{1,0:T(8,128)S(1)} collective-permute-done((f32[8,128]{1,0:T(8,128)S(1)}, f32[8,128]{1,0:T(8,128)S(1)}, u32[]{:S(2)}, u32[]{:S(2)}) %collective-permute-start.25) | collective-permute-done | bytes 4128 | tf_op jit(solution)/shard_map/ppermute | solution.py:425
  139.0 5.4 %collective-permute-start.28 = (bf16[4,64,512]{2,1,0:T(8,128)(2,1)S(1)}, bf16[4,64,512]{2,1,0:T(8,128)(2,1)S(1)}, u32[]{:S(2)}, u32[]{:S(2)}) collective-permute-start(bf16[4,64,512]{2,1,0:T(8,128)(2,1)S(1)} %get-tuple-element.95), channel_id=1, source_target_pairs={{0,1},{1,0},{2,3},{3,2},{4,5},{5,4},{6,7},{7,6},{8,9},{9,8},{10,11... | collective-permute-start | bytes 786440 | tf_op jit(solution)/shard_map/ppermute | solution.py:425
  145.6 1.4 shard_map.202
  (93 shorter events, 23.9 us)
Async XLA Ops:
  4.6 20.9 %copy-start = (s32[3]{0:T(128)S(1)}, s32[3]{0:T(128)}, u32[]{:S(2)}) copy-start(s32[3]{0:T(128)} %pad_add_fusion.idx) | copy-start | bytes 40
  4.6 20.9 %collective-permute-start = (bf16[272,1024]{1,0:T(8,128)(2,1)}, bf16[272,1024]{1,0:T(8,128)(2,1)S(1)}, u32[]{:S(2)}, u32[]{:S(2)}) collective-permute-start(bf16[272,1024]{1,0:T(8,128)(2,1)} %get-tuple-element.56), channel_id=1, source_target_pairs={{0,8},{8,16},{16,24},{24,32},{32,40},{40,48},{48,56},{56,64},{64,7... | collective-permute-start | bytes 1671176 | tf_op jit(solution)/shard_map/ppermute | solution.py:434
  8.7 16.7 %collective-permute-start.2 = (bf16[256,1024]{1,0:T(8,128)(2,1)}, bf16[256,1024]{1,0:T(8,128)(2,1)S(1)}, u32[]{:S(2)}, u32[]{:S(2)}) collective-permute-start(bf16[256,1024]{1,0:T(8,128)(2,1)} %get-tuple-element.58), channel_id=1, source_target_pairs={{8,0},{16,8},{24,16},{32,24},{40,32},{48,40},{56,48},{64,56},{72,6... | collective-permute-start | bytes 1572872 | tf_op jit(solution)/shard_map/ppermute | solution.py:434
  10.0 6.8 %collective-permute-start.3 = (bf16[272,512]{1,0:T(8,128)(2,1)}, bf16[272,512]{1,0:T(8,128)(2,1)S(1)}, u32[]{:S(2)}, u32[]{:S(2)}) collective-permute-start(bf16[272,512]{1,0:T(8,128)(2,1)} %get-tuple-element.60), channel_id=1, source_target_pairs={{0,1},{1,0},{2,3},{3,2},{4,5},{5,4},{6,7},{7,6},{8,9},{9,8},{10,11... | collective-permute-start | bytes 835592 | tf_op jit(solution)/shard_map/ppermute | solution.py:425
  11.1 10.7 %collective-permute-start.1 = (bf16[32,1024]{1,0:T(8,128)(2,1)}, bf16[32,1024]{1,0:T(8,128)(2,1)S(1)}, u32[]{:S(2)}, u32[]{:S(2)}) collective-permute-start(bf16[32,1024]{1,0:T(8,128)(2,1)} %get-tuple-element.57), channel_id=1, source_target_pairs={{0,16},{8,24},{16,32},{24,40},{32,48},{40,56},{48,64},{56,72},{64,... | collective-permute-start | bytes 196616 | tf_op jit(solution)/shard_map/ppermute | solution.py:434
  18.0 5.0 %collective-permute-start.6 = (f32[8,128]{1,0:T(8,128)S(1)}, f32[8,128]{1,0:T(8,128)S(1)}, u32[]{:S(2)}, u32[]{:S(2)}) collective-permute-start(f32[8,128]{1,0:T(8,128)S(1)} %shard_map.187.s0), channel_id=1, source_target_pairs={{0,4},{2,6},{4,0},{6,2},{1,5},{3,7},{5,1},{7,3},{8,12},{10,14},{12... | collective-permute-start | bytes 12296 | tf_op jit(solution)/shard_map/ppermute | solution.py:425
  21.0 2.8 %collective-permute-start.5 = (f32[8,128]{1,0:T(8,128)S(1)}, f32[8,128]{1,0:T(8,128)S(1)}, u32[]{:S(2)}, u32[]{:S(2)}) collective-permute-start(f32[8,128]{1,0:T(8,128)S(1)} %shard_map.187.s0), channel_id=1, source_target_pairs={{0,6},{2,0},{4,2},{6,4},{1,7},{3,1},{5,3},{7,5},{8,14},{10,8},{12,... | collective-permute-start | bytes 12296 | tf_op jit(solution)/shard_map/ppermute | solution.py:425
  21.8 3.7 %collective-permute-start.4 = (f32[8,128]{1,0:T(8,128)S(1)}, f32[8,128]{1,0:T(8,128)S(1)}, u32[]{:S(2)}, u32[]{:S(2)}) collective-permute-start(f32[8,128]{1,0:T(8,128)S(1)} %shard_map.187.s0), channel_id=1, source_target_pairs={{0,2},{2,4},{4,6},{6,0},{1,3},{3,5},{5,7},{7,1},{8,10},{10,12},{12... | collective-permute-start | bytes 12296 | tf_op jit(solution)/shard_map/ppermute | solution.py:425
  27.7 26.5 %all-to-all-start = ((bf16[8,256,128]{2,1,0:T(8,128)(2,1)}), bf16[8,256,128]{2,1,0:T(8,128)(2,1)S(1)}, u32[]{:S(2)}, u32[]{:S(2)}) async-start(bf16[8,256,128]{2,1,0:T(8,128)(2,1)} %get-tuple-element.66), calls=%async_computation | async-start | bytes 1048576 | tf_op jit(solution)/shard_map/all_to_all | solution.py:482
  54.9 5.3 %collective-permute-start.10 = (bf16[1024,128]{1,0:T(8,128)(2,1)S(1)}, bf16[1024,128]{1,0:T(8,128)(2,1)S(1)}, u32[]{:S(2)}, u32[]{:S(2)}) collective-permute-start(bf16[1024,128]{1,0:T(8,128)(2,1)S(1)} %shard_map.190.a), channel_id=1, source_target_pairs={{0,24},{8,0},{16,8},{24,16},{1,25},{9,1},{17,9},{25,17},{2,26},{10... | collective-permute-start | bytes 786440 | tf_op jit(solution)/shard_map/ppermute | solution.py:425
  56.3 9.9 %collective-permute-start.9 = (bf16[1024,128]{1,0:T(8,128)(2,1)S(1)}, bf16[1024,128]{1,0:T(8,128)(2,1)S(1)}, u32[]{:S(2)}, u32[]{:S(2)}) collective-permute-start(bf16[1024,128]{1,0:T(8,128)(2,1)S(1)} %shard_map.190.a), channel_id=1, source_target_pairs={{0,8},{8,16},{16,24},{24,0},{1,9},{9,17},{17,25},{25,1},{2,10},{10... | collective-permute-start | bytes 786440 | tf_op jit(solution)/shard_map/ppermute | solution.py:425
  56.5 9.7 %collective-permute-start.8 = (bf16[1024,128]{1,0:T(8,128)(2,1)S(1)}, bf16[1024,128]{1,0:T(8,128)(2,1)S(1)}, u32[]{:S(2)}, u32[]{:S(2)}) collective-permute-start(bf16[1024,128]{1,0:T(8,128)(2,1)S(1)} %shard_map.190.a), channel_id=1, source_target_pairs={{0,16},{8,24},{16,0},{24,8},{1,17},{9,25},{17,1},{25,9},{2,18},{10... | collective-permute-start | bytes 786440 | tf_op jit(solution)/shard_map/ppermute | solution.py:425
  66.8 8.2 %collective-permute-start.14 = (bf16[4,1024,128]{2,1,0:T(8,128)(2,1)S(1)}, bf16[4,1024,128]{2,1,0:T(8,128)(2,1)S(1)}, u32[]{:S(2)}, u32[]{:S(2)}) collective-permute-start(bf16[4,1024,128]{2,1,0:T(8,128)(2,1)S(1)} %get-tuple-element.73.mine), channel_id=1, source_target_pairs={{0,1},{1,0},{2,3},{3,2},{4,5},{5,4},{6,7},{7,6},{8,9},{9,8},{10,11... | collective-permute-start | bytes 3145736 | tf_op jit(solution)/shard_map/ppermute | solution.py:425
  81.2 8.5 %collective-permute-start.16 = (bf16[4112,128]{1,0:T(8,128)(2,1)S(1)}, bf16[4112,128]{1,0:T(8,128)(2,1)S(1)}, u32[]{:S(2)}, u32[]{:S(2)}) collective-permute-start(bf16[4112,128]{1,0:T(8,128)(2,1)S(1)} %get-tuple-element.77), channel_id=1, source_target_pairs={{0,1},{1,0},{2,3},{3,2},{4,5},{5,4},{6,7},{7,6},{8,9},{9,8},{10,11... | collective-permute-start | bytes 3158024 | tf_op jit(solution)/shard_map/ppermute | solution.py:425
  81.6 7.6 %collective-permute-start.11 = (bf16[8,48,128]{2,1,0:T(8,128)(2,1)S(1)}, bf16[8,48,128]{2,1,0:T(8,128)(2,1)S(1)}, u32[]{:S(2)}, u32[]{:S(2)}) collective-permute-start(bf16[8,48,128]{2,1,0:T(8,128)(2,1)S(1)} %get-tuple-element.70), channel_id=1, source_target_pairs={{0,8},{8,16},{16,24},{24,0},{1,9},{9,17},{17,25},{25,1},{2,10},{10... | collective-permute-start | bytes 294920 | tf_op jit(solution)/shard_map/ppermute | solution.py:425
  81.6 7.6 %collective-permute-start.12 = (bf16[8,48,128]{2,1,0:T(8,128)(2,1)S(1)}, bf16[8,48,128]{2,1,0:T(8,128)(2,1)S(1)}, u32[]{:S(2)}, u32[]{:S(2)}) collective-permute-start(bf16[8,48,128]{2,1,0:T(8,128)(2,1)S(1)} %get-tuple-element.71), channel_id=1, source_target_pairs={{0,16},{8,24},{16,0},{24,8},{1,17},{9,25},{17,1},{25,9},{2,18},{10... | collective-permute-start | bytes 294920 | tf_op jit(solution)/shard_map/ppermute | solution.py:425
  83.4 6.1 %collective-permute-start.13 = (bf16[8,48,128]{2,1,0:T(8,128)(2,1)S(1)}, bf16[8,48,128]{2,1,0:T(8,128)(2,1)S(1)}, u32[]{:S(2)}, u32[]{:S(2)}) collective-permute-start(bf16[8,48,128]{2,1,0:T(8,128)(2,1)S(1)} %get-tuple-element.72), channel_id=1, source_target_pairs={{0,24},{8,0},{16,8},{24,16},{1,25},{9,1},{17,9},{25,17},{2,26},{10... | collective-permute-start | bytes 294920 | tf_op jit(solution)/shard_map/ppermute | solution.py:425
  89.6 3.6 %collective-permute-start.15 = (bf16[8,48,128]{2,1,0:T(8,128)(2,1)S(1)}, bf16[8,48,128]{2,1,0:T(8,128)(2,1)S(1)}, u32[]{:S(2)}, u32[]{:S(2)}) collective-permute-start(bf16[8,48,128]{2,1,0:T(8,128)(2,1)S(1)} %get-tuple-element.75.a), channel_id=1, source_target_pairs={{0,32},{32,0},{64,96},{96,64},{128,160},{160,128},{192,224},{224,1... | collective-permute-start | bytes 294920 | tf_op jit(solution)/shard_map/ppermute | solution.py:429
  93.7 7.4 %collective-permute-start.17 = (bf16[8,48,128]{2,1,0:T(8,128)(2,1)S(1)}, bf16[8,48,128]{2,1,0:T(8,128)(2,1)S(1)}, u32[]{:S(2)}, u32[]{:S(2)}) collective-permute-start(bf16[8,48,128]{2,1,0:T(8,128)(2,1)S(1)} %get-tuple-element.80.a), channel_id=1, source_target_pairs={{0,128},{32,160},{64,192},{96,224},{128,0},{160,32},{192,64},{224,... | collective-permute-start | bytes 294920 | tf_op jit(solution)/shard_map/ppermute | solution.py:429
  96.9 10.2 %collective-permute-start.22 = (bf16[1040,128]{1,0:T(8,128)(2,1)S(1)}, bf16[1040,128]{1,0:T(8,128)(2,1)S(1)}, u32[]{:S(2)}, u32[]{:S(2)}) collective-permute-start(bf16[1040,128]{1,0:T(8,128)(2,1)S(1)} %get-tuple-element.86), channel_id=1, source_target_pairs={{0,8},{8,16},{16,24},{24,0},{1,9},{9,17},{17,25},{25,1},{2,10},{10... | collective-permute-start | bytes 798728 | tf_op jit(solution)/shard_map/ppermute | solution.py:425
  97.2 10.0 %collective-permute-start.23 = (bf16[1040,128]{1,0:T(8,128)(2,1)S(1)}, bf16[1040,128]{1,0:T(8,128)(2,1)S(1)}, u32[]{:S(2)}, u32[]{:S(2)}) collective-permute-start(bf16[1040,128]{1,0:T(8,128)(2,1)S(1)} %get-tuple-element.87), channel_id=1, source_target_pairs={{0,24},{8,0},{16,8},{24,16},{1,25},{9,1},{17,9},{25,17},{2,26},{10... | collective-permute-start | bytes 798728 | tf_op jit(solution)/shard_map/ppermute | solution.py:425
  99.6 11.0 %collective-permute-start.24 = (bf16[1040,128]{1,0:T(8,128)(2,1)S(1)}, bf16[1040,128]{1,0:T(8,128)(2,1)S(1)}, u32[]{:S(2)}, u32[]{:S(2)}) collective-permute-start(bf16[1040,128]{1,0:T(8,128)(2,1)S(1)} %get-tuple-element.88), channel_id=1, source_target_pairs={{0,16},{8,24},{16,0},{24,8},{1,17},{9,25},{17,1},{25,9},{2,18},{10... | collective-permute-start | bytes 798728 | tf_op jit(solution)/shard_map/ppermute | solution.py:425
  101.7 5.4 %collective-permute-start.18 = (bf16[8,48,128]{2,1,0:T(8,128)(2,1)S(1)}, bf16[8,48,128]{2,1,0:T(8,128)(2,1)S(1)}, u32[]{:S(2)}, u32[]{:S(2)}) collective-permute-start(bf16[8,48,128]{2,1,0:T(8,128)(2,1)S(1)} %get-tuple-element.81.a), channel_id=1, source_target_pairs={{0,64},{32,96},{64,0},{96,32},{128,192},{160,224},{192,128},{224,1... | collective-permute-start | bytes 294920 | tf_op jit(solution)/shard_map/ppermute | solution.py:429
  111.6 18.6 %all-to-all-start.1 = ((bf16[8,272,128]{2,1,0:T(8,128)(2,1)}), bf16[8,272,128]{2,1,0:T(8,128)(2,1)S(1)}, u32[]{:S(2)}, u32[]{:S(2)}) async-start(bf16[8,272,128]{2,1,0:T(8,128)(2,1)} %get-tuple-element.91), calls=%async_computation.1 | async-start | bytes 1114112 | tf_op jit(solution)/shard_map/all_to_all | solution.py:568
  115.2 5.1 %collective-permute-start.21 = (bf16[8,48,128]{2,1,0:T(8,128)(2,1)S(1)}, bf16[8,48,128]{2,1,0:T(8,128)(2,1)S(1)}, u32[]{:S(2)}, u32[]{:S(2)}) collective-permute-start(bf16[8,48,128]{2,1,0:T(8,128)(2,1)S(1)} %get-tuple-element.82.p0), channel_id=1, source_target_pairs={{0,16},{8,24},{16,0},{24,8},{1,17},{9,25},{17,1},{25,9},{2,18},{10... | collective-permute-start | bytes 294920 | tf_op jit(solution)/shard_map/ppermute | solution.py:425
  115.3 5.2 %collective-permute-start.20 = (bf16[8,48,128]{2,1,0:T(8,128)(2,1)S(1)}, bf16[8,48,128]{2,1,0:T(8,128)(2,1)S(1)}, u32[]{:S(2)}, u32[]{:S(2)}) collective-permute-start(bf16[8,48,128]{2,1,0:T(8,128)(2,1)S(1)} %get-tuple-element.82.p0), channel_id=1, source_target_pairs={{0,24},{8,0},{16,8},{24,16},{1,25},{9,1},{17,9},{25,17},{2,26},{10... | collective-permute-start | bytes 294920 | tf_op jit(solution)/shard_map/ppermute | solution.py:425
  118.3 4.7 %collective-permute-start.19 = (bf16[8,48,128]{2,1,0:T(8,128)(2,1)S(1)}, bf16[8,48,128]{2,1,0:T(8,128)(2,1)S(1)}, u32[]{:S(2)}, u32[]{:S(2)}) collective-permute-start(bf16[8,48,128]{2,1,0:T(8,128)(2,1)S(1)} %get-tuple-element.82.p0), channel_id=1, source_target_pairs={{0,8},{8,16},{16,24},{24,0},{1,9},{9,17},{17,25},{25,1},{2,10},{10... | collective-permute-start | bytes 294920 | tf_op jit(solution)/shard_map/ppermute | solution.py:425
  118.3 17.0 %collective-permute-start.7 = (bf16[3,16,1024]{2,1,0:T(8,128)(2,1)S(1)}, bf16[3,16,1024]{2,1,0:T(8,128)(2,1)S(1)}, u32[]{:S(2)}, u32[]{:S(2)}) collective-permute-start(bf16[3,16,1024]{2,1,0:T(8,128)(2,1)S(1)} %copy-done.15), channel_id=1, source_target_pairs={{8,0},{16,8},{24,16},{32,24},{40,32},{48,40},{56,48},{64,56},{72,6... | collective-permute-start | bytes 294920 | tf_op jit(solution)/shard_map/ppermute | solution.py:434
  131.5 4.0 %collective-permute-start.27 = (f32[8,128]{1,0:T(8,128)S(1)}, f32[8,128]{1,0:T(8,128)S(1)}, u32[]{:S(2)}, u32[]{:S(2)}) collective-permute-start(f32[8,128]{1,0:T(8,128)S(1)} %get-tuple-element.93.p0), channel_id=1, source_target_pairs={{0,4},{2,6},{4,0},{6,2},{1,5},{3,7},{5,1},{7,3},{8,12},{10,14},{12... | collective-permute-start | bytes 12296 | tf_op jit(solution)/shard_map/ppermute | solution.py:425
  133.8 2.5 %collective-permute-start.26 = (f32[8,128]{1,0:T(8,128)S(1)}, f32[8,128]{1,0:T(8,128)S(1)}, u32[]{:S(2)}, u32[]{:S(2)}) collective-permute-start(f32[8,128]{1,0:T(8,128)S(1)} %get-tuple-element.93.p0), channel_id=1, source_target_pairs={{0,6},{2,0},{4,2},{6,4},{1,7},{3,1},{5,3},{7,5},{8,14},{10,8},{12,... | collective-permute-start | bytes 12296 | tf_op jit(solution)/shard_map/ppermute | solution.py:425
  134.6 3.7 %collective-permute-start.25 = (f32[8,128]{1,0:T(8,128)S(1)}, f32[8,128]{1,0:T(8,128)S(1)}, u32[]{:S(2)}, u32[]{:S(2)}) collective-permute-start(f32[8,128]{1,0:T(8,128)S(1)} %get-tuple-element.93.p0), channel_id=1, source_target_pairs={{0,2},{2,4},{4,6},{6,0},{1,3},{3,5},{5,7},{7,1},{8,10},{10,12},{12... | collective-permute-start | bytes 12296 | tf_op jit(solution)/shard_map/ppermute | solution.py:425
  139.0 6.6 %collective-permute-start.28 = (bf16[4,64,512]{2,1,0:T(8,128)(2,1)S(1)}, bf16[4,64,512]{2,1,0:T(8,128)(2,1)S(1)}, u32[]{:S(2)}, u32[]{:S(2)}) collective-permute-start(bf16[4,64,512]{2,1,0:T(8,128)(2,1)S(1)} %get-tuple-element.95), channel_id=1, source_target_pairs={{0,1},{1,0},{2,3},{3,2},{4,5},{5,4},{6,7},{7,6},{8,9},{9,8},{10,11... | collective-permute-start | bytes 786440 | tf_op jit(solution)/shard_map/ppermute | solution.py:425
  (15 other events, 108.1 us)
where the time goes:
time: 147 us
  starting transfers between devices  65.5 us (45%)
  waiting for transfers between devices  44.7 us (30%)
  Pallas kernels  31.6 us (21%)
  local copies, waits for them, and re-layouts  2.47 us (2%)
  other arithmetic  1.67 us (1%)
    ppermute x22, starting transfers between devices, rotate(): return lax.ppermute(x, axis, [(i, (i + by) % size) for i in range(size)])  33.6 us
    ppermute x22, waiting for transfers between devices, rotate(): return lax.ppermute(x, axis, [(i, (i + by) % size) for i in range(size)])  28.2 us
    ppermute x4, starting transfers between devices, along(): lax.ppermute(x, ('z', 'x'), [(i, i + by) for i in range(count) if 0 <= i...  12.5 us
    all_to_all x1, starting transfers between devices, local(): blk = lax.all_to_all(payload, 'z', 0, 0)  11.9 us
    pallas_call x1, Pallas kernels, local(): call(hyena_kernel, [shape((ROWS, channels), BF16), shape((3, ROWS, channe...  11.7 us
    ppermute x3, waiting for transfers between devices, flip(): return lax.ppermute(x, axis, [(i, i ^ by) for i in range(size)])  7.88 us
    pallas_call x1, Pallas kernels, local(): call(attention_kernel, [shape((4096, 128), F32), shape((8, 128), F32), sh...  6.13 us
    all_to_all x1, waiting for transfers between devices, local(): back = lax.all_to_all(outgoing, 'z', 0, 0)  5.75 us
  transfers between devices with their start and end apart: 31, of which 19 were waited for; matrix products, arithmetic and copies ran while one was open for 1% of the time, Pallas kernels for 11%

commit v1 on v0

--- a/solution.py
+++ b/solution.py
@@ -166,7 +166,7 @@
     return high, mid, x - high - mid
 
 
-def halves_kernel(idx, keys, values, queries, grads, streams, hg, gq, gk, mine, send, to_next, to_prev, to_second, sems):
+def halves_kernel(idx, keys, values, queries, grads, streams, hg, gq, gk, mine, send, to_next, to_prev, to_second, own_sums, sems):
     core = idx[1]
     here = pl.multiple_of(core * HALF, HALF)
     there = pl.multiple_of((1 - core) * HALF, HALF)
@@ -192,6 +192,7 @@
     send[256:272] = jnp.concatenate(parts, 0).astype(BF16)
     for c in copies:
         c.wait()
+    own_sums[...] = squares_of(mine)
 
 
 def own_gains(gn_q, gn_k):
@@ -203,16 +204,20 @@
     return wide[0:2] + wide[2:4] + wide[4:6]
 
 
-def square_kernel(mine, other, out):
+def squares_of(rows):
     sums = []
     for slot in (2, 0):
-        at = slice(slot * HALF, slot * HALF + HALF)
-        a, b = mine[at].astype(F32), other[at].astype(F32)
-        sums.append(lane_sum(a * a + b * b))
-    out[...] = to_lanes(sums[0], sums[1])
-
-
-def pack_kernel(idx, mine, other, gn_q, gn_k, s0, s1, s2, s3, h0, h1, h2, out, rates):
+        wide = rows[slot * HALF : slot * HALF + HALF].astype(F32)
+        sums.append(lane_sum(wide * wide))
+    return to_lanes(sums[0], sums[1])
+
+
+def square_kernel(own_sums, other, out):
+    out[...] = own_sums[...] + squares_of(other)
+
+
+def pack_kernel(idx, mine, other, gn_q, gn_k, s0, s1, s2, s3, h0, h1, h2, out, rates, done):
+    done[...] = jnp.zeros((8, 128), F32)
     core = idx[1]
     rate = lax.rsqrt((s0[...] + s1[...] + s2[...] + s3[...]) / (NY * 8 * HD) + EPS)
     rates[...] = rate
@@ -453,15 +458,15 @@
     tab = jnp.asarray(transform_tables())
     st = streams.transpose(1, 0, 2)
     sf = short_filter.transpose(1, 0, 2)
-    mine, send, to_next, to_prev, to_second = call(
+    mine, send, to_next, to_prev, to_second, own_sums = call(
         halves_kernel,
         [
             shape((256, 512), BF16), shape((272, 512), BF16), shape((272, channels), BF16),
-            shape((256, channels), BF16), shape((32, channels), BF16),
+            shape((256, channels), BF16), shape((32, channels), BF16), shape((8, 128), F32),
         ],
         [pltpu.SemaphoreType.DMA((15,))],
         in_specs=[SM] + [ANY] * 6 + [VM] * 2,
-        out_specs=[VM] * 5,
+        out_specs=[VM] * 6,
         us=1.0,
         vmem=60,
     )(idx, keys, values, queries, attn_grad, st, hyena_grad, *gains)
@@ -470,13 +475,13 @@
     prev = along(to_next, 1)
     following = along(to_prev, -1)
 
-    squares = call(square_kernel, shape((8, 128), F32), in_specs=[VM, VM], out_specs=VM, us=0.7)(mine, other)
+    squares = call(square_kernel, shape((8, 128), F32), in_specs=[VM, VM], out_specs=VM, us=0.7)(own_sums, other)
     sums = [squares] + [rotate(squares, "y", NY, d) for d in (1, 3, 2)]
-    payload, rates = call(
+    payload, rates, packed = call(
         pack_kernel,
-        [shape((8, 256, 128), BF16), shape((8, 128), F32)],
+        [shape((8, 256, 128), BF16), shape((8, 128), F32), shape((8, 128), F32)],
         in_specs=[SM] + [VM] * 8 + [ANY] * 3,
-        out_specs=[VM, VM],
+        out_specs=[VM] * 3,
         us=1.5,
     )(idx, mine, other, *gains, *sums, prev, following, second)
     blk = lax.all_to_all(payload, "z", 0, 0)
@@ -512,7 +517,7 @@
             spec(128), spec(3, 128), spec(3, 16), spec(3, 16), pl.BlockSpec((NX, 2, 48, 128), lambda i: (0, i, 0, 0)), VM,
         ],
         us=11.0, vmem=56,
-    )(st, prev, second, following, hyena_grad, sf, long_filter, tab, rates)
+    )(st, prev, second, following, hyena_grad, sf, long_filter, tab, packed)
     next_head = along(head, -1)
 
     kv = call(
@@ -556,7 +561,7 @@
         us=1.0,
     )(idx, keep, gkeep, from_core, scattered)
     rest = [rotate(s, "x", NX, d) for d, s in ((1, s1), (3, s3), (2, s2))]
-    for by in (1, 4, 2):
+    for by in (1, 2, 4):
         piece, added = call(
             pair_sum_kernel, [piece_shape, token], in_specs=[VM] * 2 + [ANY], out_specs=[VM] * 2, us=0.6
         )(piece, flip(piece, "z", NZ, by), g0)

time: 147 us -> 146 us (level)
  waiting for transfers between devices: 44.7 us -> 39.4 us
  starting transfers between devices: 65.5 us -> 69.8 us
    ppermute x22, waiting for transfers between devices: 28.2 us -> 25.3 us  [rotate(): return lax.ppermute(x, axis, [(i, (i + by) % size) for i in range(size)])]
    ppermute x22, starting transfers between devices: 33.6 us -> 36.3 us  [rotate(): return lax.ppermute(x, axis, [(i, (i + by) % size) for i in range(size)])]
    all_to_all x1, waiting for transfers between devices: 5.75 us -> 3.61 us  [local(): back = lax.all_to_all(outgoing, 'z', 0, 0)]
  transfers between devices with their start and end apart: 31 -> 31, of which waited for: 19 -> 21; matrix products, arithmetic and copies ran while one was open for 1% -> 1% of each run, Pallas kernels for 11% -> 11%
where the time goes in v1:
time: 146 us
  starting transfers between devices  69.8 us (48%)
  waiting for transfers between devices  39.4 us (27%)
  Pallas kernels  31.6 us (22%)
  local copies, waits for them, and re-layouts  2.2 us (2%)
  other arithmetic  1.67 us (1%)
    ppermute x22, starting transfers between devices, rotate(): return lax.ppermute(x, axis, [(i, (i + by) % size) for i in range(size)])  36.3 us
    ppermute x22, waiting for transfers between devices, rotate(): return lax.ppermute(x, axis, [(i, (i + by) % size) for i in range(size)])  25.3 us
    ppermute x4, starting transfers between devices, along(): lax.ppermute(x, ('z', 'x'), [(i, i + by) for i in range(count) if 0 <= i...  12.5 us
    all_to_all x1, starting transfers between devices, local(): blk = lax.all_to_all(payload, 'z', 0, 0)  11.9 us
    pallas_call x1, Pallas kernels, local(): call(hyena_kernel, [shape((ROWS, channels), BF16), shape((3, ROWS, channe...  11.8 us
    ppermute x3, waiting for transfers between devices, flip(): return lax.ppermute(x, axis, [(i, i ^ by) for i in range(size)])  7.46 us
    pallas_call x1, Pallas kernels, local(): call(attention_kernel, [shape((4096, 128), F32), shape((8, 128), F32), sh...  6.13 us
    all_to_all x1, starting transfers between devices, local(): back = lax.all_to_all(outgoing, 'z', 0, 0)  4.91 us
  transfers between devices with their start and end apart: 31, of which 21 were waited for; matrix products, arithmetic and copies ran while one was open for 1% of the time, Pallas kernels for 11%

profile of v1, /device:TPU:1, one launch (start us, length us, event | category | flops | bytes accessed | tf_op | source)
XLA Modules:
  0.0 145.6 jit_solution(15881690439501718556)
XLA Ops:
  1.2 3.3 %shard_map.186 = (bf16[256,512]{1,0:T(8,128)(2,1)}, bf16[272,512]{1,0:T(8,128)(2,1)}, bf16[272,1024]{1,0:T(8,128)(2,1)}, bf16[256,1024]{1,0:T(8,128)(2,1)}, bf16[32,1024]{1,0:T(8,128)(2,1)}, /*index=5*/f32[8,128]{1,0:T(8,128)}) custom-call(s32[3]{0:T(128)} %pad_add_fusion.idx, bf16[128,512]{1,0:T(8,128)(2,1)} %keys.1, bf16[128,512]{1,0:T(8,128)(2,1)} %values.1, ...), custom_call_target="tpu_custom_call" | custom-call | flops 1100000000 | tf_op jit(solution)/shard_map/pallas_call | solution.py:461
  4.6 4.1 %collective-permute-start = (bf16[272,1024]{1,0:T(8,128)(2,1)}, bf16[272,1024]{1,0:T(8,128)(2,1)S(1)}, u32[]{:S(2)}, u32[]{:S(2)}) collective-permute-start(bf16[272,1024]{1,0:T(8,128)(2,1)} %get-tuple-element.58), channel_id=1, source_target_pairs={{0,8},{8,16},{16,24},{24,32},{32,40},{40,48},{48,56},{56,64},{64,7... | collective-permute-start | bytes 1671176 | tf_op jit(solution)/shard_map/ppermute | solution.py:439
  8.8 1.3 collective-permute-start.2
  11.1 5.8 %collective-permute-start.1 = (bf16[32,1024]{1,0:T(8,128)(2,1)}, bf16[32,1024]{1,0:T(8,128)(2,1)S(1)}, u32[]{:S(2)}, u32[]{:S(2)}) collective-permute-start(bf16[32,1024]{1,0:T(8,128)(2,1)} %get-tuple-element.59), channel_id=1, source_target_pairs={{0,16},{8,24},{16,32},{24,40},{32,48},{40,56},{48,64},{56,72},{64,... | collective-permute-start | bytes 196616 | tf_op jit(solution)/shard_map/ppermute | solution.py:439
  17.8 3.0 %collective-permute-start.6 = (f32[8,128]{1,0:T(8,128)S(1)}, f32[8,128]{1,0:T(8,128)S(1)}, u32[]{:S(2)}, u32[]{:S(2)}) collective-permute-start(f32[8,128]{1,0:T(8,128)S(1)} %shard_map.187.s0), channel_id=1, source_target_pairs={{0,4},{2,6},{4,0},{6,2},{1,5},{3,7},{5,1},{7,3},{8,12},{10,14},{12... | collective-permute-start | bytes 12296 | tf_op jit(solution)/shard_map/ppermute | solution.py:430
  21.7 1.3 collective-permute-start.4
  23.5 1.9 %collective-permute-done.4.s1 = f32[8,128]{1,0:T(8,128)S(1)} collective-permute-done((f32[8,128]{1,0:T(8,128)S(1)}, f32[8,128]{1,0:T(8,128)S(1)}, u32[]{:S(2)}, u32[]{:S(2)}) %collective-permute-start.4) | collective-permute-done | bytes 4128 | tf_op jit(solution)/shard_map/ppermute | solution.py:430
  25.5 1.6 %shard_map.188 = (bf16[8,256,128]{2,1,0:T(8,128)(2,1)}, f32[8,128]{1,0:T(8,128)S(1)}, f32[8,128]{1,0:T(8,128)S(1)}) custom-call(s32[3]{0:T(128)S(1)} %copy-done, bf16[256,512]{1,0:T(8,128)(2,1)S(1)} %copy-done.7, bf16[272,512]{1,0:T(8,128)(2,1)S(1)} %collective-permute-done.3.other, f32[1,512]{1,0:T(1,128)S(1)} %bitcast.25, f32[1,512]{1,0:T(1,128)S(1)} %bitcast.29, ...), custom_call_target="tpu_custom_call" | custom-call | flops 1650000000 | tf_op jit(solution)/shard_map/pallas_call | solution.py:480
  27.7 11.9 %all-to-all-start = ((bf16[8,256,128]{2,1,0:T(8,128)(2,1)}), bf16[8,256,128]{2,1,0:T(8,128)(2,1)S(1)}, u32[]{:S(2)}, u32[]{:S(2)}) async-start(bf16[8,256,128]{2,1,0:T(8,128)(2,1)} %get-tuple-element.69), calls=%async_computation | async-start | bytes 1048576 | tf_op jit(solution)/shard_map/all_to_all | solution.py:487
  39.6 11.8 %shard_map.189 = (bf16[128,1024]{1,0:T(8,128)(2,1)}, bf16[3,128,1024]{2,1,0:T(8,128)(2,1)}, bf16[3,16,1024]{2,1,0:T(8,128)(2,1)}, f32[3,16,1024]{2,1,0:T(8,128)}...) custom-call(bf16[3,128,1024]{2,1,0:T(8,128)(2,1)} %bitcast.35, bf16[272,1024]{1,0:T(8,128)(2,1)} %copy-done.1, ...), custom_call_target="tpu_custom_call" | custom-call | flops 12099999744 | tf_op jit(solution)/shard_map/pallas_call | solution.py:500
  51.4 2.9 %all-to-all-done.blk = bf16[8,256,128]{2,1,0:T(8,128)(2,1)S(1)} async-done(((bf16[8,256,128]{2,1,0:T(8,128)(2,1)}), bf16[8,256,128]{2,1,0:T(8,128)(2,1)S(1)}, u32[]{:S(2)}, u32[]{:S(2)}) %all-to-all-start) | async-done | bytes 524320 | tf_op jit(solution)/shard_map/all_to_all | solution.py:487
  55.0 1.4 collective-permute-start.10
  57.6 2.7 %collective-permute-done.10.d = bf16[1024,128]{1,0:T(8,128)(2,1)S(1)} collective-permute-done((bf16[1024,128]{1,0:T(8,128)(2,1)S(1)}, bf16[1024,128]{1,0:T(8,128)(2,1)S(1)}, u32[]{:S(2)}, u32[]{:S(2)}) %collective-permute-start.10) | collective-permute-done | bytes 262176 | tf_op jit(solution)/shard_map/ppermute | solution.py:430
  60.3 5.9 %collective-permute-done.9.b = bf16[1024,128]{1,0:T(8,128)(2,1)S(1)} collective-permute-done((bf16[1024,128]{1,0:T(8,128)(2,1)S(1)}, bf16[1024,128]{1,0:T(8,128)(2,1)S(1)}, u32[]{:S(2)}, u32[]{:S(2)}) %collective-permute-start.9) | collective-permute-done | bytes 262176 | tf_op jit(solution)/shard_map/ppermute | solution.py:430
  66.8 6.0 %collective-permute-start.14 = (bf16[4,1024,128]{2,1,0:T(8,128)(2,1)S(1)}, bf16[4,1024,128]{2,1,0:T(8,128)(2,1)S(1)}, u32[]{:S(2)}, u32[]{:S(2)}) collective-permute-start(bf16[4,1024,128]{2,1,0:T(8,128)(2,1)S(1)} %get-tuple-element.76.mine), channel_id=1, source_target_pairs={{0,1},{1,0},{2,3},{3,2},{4,5},{5,4},{6,7},{7,6},{8,9},{9,8},{10,11... | collective-permute-start | bytes 3145736 | tf_op jit(solution)/shard_map/ppermute | solution.py:430
  72.8 2.3 %collective-permute-done.14.pair = bf16[4,1024,128]{2,1,0:T(8,128)(2,1)S(1)} collective-permute-done((bf16[4,1024,128]{2,1,0:T(8,128)(2,1)S(1)}, bf16[4,1024,128]{2,1,0:T(8,128)(2,1)S(1)}, u32[]{:S(2)}, u32[]{:S(2)}) %collective-permute-start.14) | collective-permute-done | bytes 1048608 | tf_op jit(solution)/shard_map/ppermute | solution.py:430
  75.1 6.1 %shard_map.192 = (f32[4096,128]{1,0:T(8,128)S(1)}, f32[8,128]{1,0:T(8,128)S(1)}, bf16[4112,128]{1,0:T(8,128)(2,1)S(1)}, bf16[8,128,128]{2,1,0:T(8,128)(2,1)S(1)}) custom-call(s32[3]{0:T(128)S(1)} %copy-done, bf16[8,256,128]{2,1,0:T(8,128)(2,1)S(1)} %all-to-all-done.blk, bf16[4,1024,128]{2,1,0:T(8,128)(2,1)S(1)} %get-tuple-element.76.mine, ...), custom_call_target="tpu_custom_call" | custom-call | flops 7699999744 | tf_op jit(solution)/shard_map/pallas_call | solution.py:535
  81.7 1.7 %collective-permute-start.12 = (bf16[8,48,128]{2,1,0:T(8,128)(2,1)S(1)}, bf16[8,48,128]{2,1,0:T(8,128)(2,1)S(1)}, u32[]{:S(2)}, u32[]{:S(2)}) collective-permute-start(bf16[8,48,128]{2,1,0:T(8,128)(2,1)S(1)} %get-tuple-element.74), channel_id=1, source_target_pairs={{0,16},{8,24},{16,0},{24,8},{1,17},{9,25},{17,1},{25,9},{2,18},{10... | collective-permute-start | bytes 294920 | tf_op jit(solution)/shard_map/ppermute | solution.py:430
  84.3 4.9 %collective-permute-done.11.p1 = bf16[8,48,128]{2,1,0:T(8,128)(2,1)S(1)} collective-permute-done((bf16[8,48,128]{2,1,0:T(8,128)(2,1)S(1)}, bf16[8,48,128]{2,1,0:T(8,128)(2,1)S(1)}, u32[]{:S(2)}, u32[]{:S(2)}) %collective-permute-start.11) | collective-permute-done | bytes 98336 | tf_op jit(solution)/shard_map/ppermute | solution.py:430
  90.4 2.7 %collective-permute-done.15.b = bf16[8,48,128]{2,1,0:T(8,128)(2,1)S(1)} collective-permute-done((bf16[8,48,128]{2,1,0:T(8,128)(2,1)S(1)}, bf16[8,48,128]{2,1,0:T(8,128)(2,1)S(1)}, u32[]{:S(2)}, u32[]{:S(2)}) %collective-permute-start.15) | collective-permute-done | bytes 98336 | tf_op jit(solution)/shard_map/ppermute | solution.py:434
  94.6 2.4 %collective-permute-start.23 = (bf16[1040,128]{1,0:T(8,128)(2,1)S(1)}, bf16[1040,128]{1,0:T(8,128)(2,1)S(1)}, u32[]{:S(2)}, u32[]{:S(2)}) collective-permute-start(bf16[1040,128]{1,0:T(8,128)(2,1)S(1)} %get-tuple-element.90), channel_id=1, source_target_pairs={{0,24},{8,0},{16,8},{24,16},{1,25},{9,1},{17,9},{25,17},{2,26},{10... | collective-permute-start | bytes 798728 | tf_op jit(solution)/shard_map/ppermute | solution.py:430
  99.5 3.5 %collective-permute-start.18 = (bf16[8,48,128]{2,1,0:T(8,128)(2,1)S(1)}, bf16[8,48,128]{2,1,0:T(8,128)(2,1)S(1)}, u32[]{:S(2)}, u32[]{:S(2)}) collective-permute-start(bf16[8,48,128]{2,1,0:T(8,128)(2,1)S(1)} %get-tuple-element.84.a), channel_id=1, source_target_pairs={{0,128},{32,160},{64,192},{96,224},{128,0},{160,32},{192,64},{224,... | collective-permute-start | bytes 294920 | tf_op jit(solution)/shard_map/ppermute | solution.py:434
  103.0 3.9 %collective-permute-done.18.b = bf16[8,48,128]{2,1,0:T(8,128)(2,1)S(1)} collective-permute-done((bf16[8,48,128]{2,1,0:T(8,128)(2,1)S(1)}, bf16[8,48,128]{2,1,0:T(8,128)(2,1)S(1)}, u32[]{:S(2)}, u32[]{:S(2)}) %collective-permute-start.18) | collective-permute-done | bytes 98336 | tf_op jit(solution)/shard_map/ppermute | solution.py:434
  108.9 4.9 %all-to-all-start.1 = ((bf16[8,272,128]{2,1,0:T(8,128)(2,1)}), bf16[8,272,128]{2,1,0:T(8,128)(2,1)S(1)}, u32[]{:S(2)}, u32[]{:S(2)}) async-start(bf16[8,272,128]{2,1,0:T(8,128)(2,1)} %get-tuple-element.94), calls=%async_computation.1 | async-start | bytes 1114112 | tf_op jit(solution)/shard_map/all_to_all | solution.py:573
  114.6 1.5 %collective-permute-start.20 = (bf16[8,48,128]{2,1,0:T(8,128)(2,1)S(1)}, bf16[8,48,128]{2,1,0:T(8,128)(2,1)S(1)}, u32[]{:S(2)}, u32[]{:S(2)}) collective-permute-start(bf16[8,48,128]{2,1,0:T(8,128)(2,1)S(1)} %get-tuple-element.85.p0), channel_id=1, source_target_pairs={{0,24},{8,0},{16,8},{24,16},{1,25},{9,1},{17,9},{25,17},{2,26},{10... | collective-permute-start | bytes 294920 | tf_op jit(solution)/shard_map/ppermute | solution.py:430
  120.7 1.5 %shard_map.198 = (f32[128,1024]{1,0:T(8,128)}, f32[3,7,1024]{2,1,0:T(8,128)}, f32[8,128]{1,0:T(8,128)S(1)}) custom-call(s32[3]{0:T(128)S(1)} %copy-done, bf16[8,48,128]{2,1,0:T(8,128)(2,1)S(1)} %get-tuple-element.85.p0, bf16[8,48,128]{2,1,0:T(8,128)(2,1)S(1)} %collective-permute-done.19.p1, bf16[8,48,128]{2,1,0:T(8,128)(2,1)S(1)} %collective-permute-done.20.p3, ...), custom_call_target="tpu_custom_call" | custom-call | flops 1100000000 | tf_op jit(solution)/shard_map/pallas_call | solution.py:576
  122.2 3.6 %all-to-all-done.1.back = bf16[8,272,128]{2,1,0:T(8,128)(2,1)S(1)} async-done(((bf16[8,272,128]{2,1,0:T(8,128)(2,1)}), bf16[8,272,128]{2,1,0:T(8,128)(2,1)S(1)}, u32[]{:S(2)}, u32[]{:S(2)}) %all-to-all-start.1) | async-done | bytes 557088 | tf_op jit(solution)/shard_map/all_to_all | solution.py:573
  125.8 1.3 shard_map.200
  127.1 1.8 %collective-permute-start.27 = (f32[8,128]{1,0:T(8,128)S(1)}, f32[8,128]{1,0:T(8,128)S(1)}, u32[]{:S(2)}, u32[]{:S(2)}) collective-permute-start(f32[8,128]{1,0:T(8,128)S(1)} %get-tuple-element.97.p0), channel_id=1, source_target_pairs={{0,4},{2,6},{4,0},{6,2},{1,5},{3,7},{5,1},{7,3},{8,12},{10,14},{12... | collective-permute-start | bytes 12296 | tf_op jit(solution)/shard_map/ppermute | solution.py:430
  131.7 1.7 %collective-permute-done.25.p1 = f32[8,128]{1,0:T(8,128)S(1)} collective-permute-done((f32[8,128]{1,0:T(8,128)S(1)}, f32[8,128]{1,0:T(8,128)S(1)}, u32[]{:S(2)}, u32[]{:S(2)}) %collective-permute-start.25) | collective-permute-done | bytes 4128 | tf_op jit(solution)/shard_map/ppermute | solution.py:430
  134.2 8.9 %collective-permute-start.28 = (bf16[4,64,512]{2,1,0:T(8,128)(2,1)S(1)}, bf16[4,64,512]{2,1,0:T(8,128)(2,1)S(1)}, u32[]{:S(2)}, u32[]{:S(2)}) collective-permute-start(bf16[4,64,512]{2,1,0:T(8,128)(2,1)S(1)} %get-tuple-element.99), channel_id=1, source_target_pairs={{0,1},{1,0},{2,3},{3,2},{4,5},{5,4},{6,7},{7,6},{8,9},{9,8},{10,11... | collective-permute-start | bytes 786440 | tf_op jit(solution)/shard_map/ppermute | solution.py:430
  144.3 1.4 shard_map.202
  (91 shorter events, 25.8 us)
Async XLA Ops:
  4.6 20.9 %copy-start = (s32[3]{0:T(128)S(1)}, s32[3]{0:T(128)}, u32[]{:S(2)}) copy-start(s32[3]{0:T(128)} %pad_add_fusion.idx) | copy-start | bytes 40
  4.6 20.8 %collective-permute-start = (bf16[272,1024]{1,0:T(8,128)(2,1)}, bf16[272,1024]{1,0:T(8,128)(2,1)S(1)}, u32[]{:S(2)}, u32[]{:S(2)}) collective-permute-start(bf16[272,1024]{1,0:T(8,128)(2,1)} %get-tuple-element.58), channel_id=1, source_target_pairs={{0,8},{8,16},{16,24},{24,32},{32,40},{40,48},{48,56},{56,64},{64,7... | collective-permute-start | bytes 1671176 | tf_op jit(solution)/shard_map/ppermute | solution.py:439
  8.8 16.7 %collective-permute-start.2 = (bf16[256,1024]{1,0:T(8,128)(2,1)}, bf16[256,1024]{1,0:T(8,128)(2,1)S(1)}, u32[]{:S(2)}, u32[]{:S(2)}) collective-permute-start(bf16[256,1024]{1,0:T(8,128)(2,1)} %get-tuple-element.60), channel_id=1, source_target_pairs={{8,0},{16,8},{24,16},{32,24},{40,32},{48,40},{56,48},{64,56},{72,6... | collective-permute-start | bytes 1572872 | tf_op jit(solution)/shard_map/ppermute | solution.py:439
  10.1 6.8 %collective-permute-start.3 = (bf16[272,512]{1,0:T(8,128)(2,1)}, bf16[272,512]{1,0:T(8,128)(2,1)S(1)}, u32[]{:S(2)}, u32[]{:S(2)}) collective-permute-start(bf16[272,512]{1,0:T(8,128)(2,1)} %get-tuple-element.62), channel_id=1, source_target_pairs={{0,1},{1,0},{2,3},{3,2},{4,5},{5,4},{6,7},{7,6},{8,9},{9,8},{10,11... | collective-permute-start | bytes 835592 | tf_op jit(solution)/shard_map/ppermute | solution.py:430
  11.1 10.6 %collective-permute-start.1 = (bf16[32,1024]{1,0:T(8,128)(2,1)}, bf16[32,1024]{1,0:T(8,128)(2,1)S(1)}, u32[]{:S(2)}, u32[]{:S(2)}) collective-permute-start(bf16[32,1024]{1,0:T(8,128)(2,1)} %get-tuple-element.59), channel_id=1, source_target_pairs={{0,16},{8,24},{16,32},{24,40},{32,48},{40,56},{48,64},{56,72},{64,... | collective-permute-start | bytes 196616 | tf_op jit(solution)/shard_map/ppermute | solution.py:439
  17.8 5.2 %collective-permute-start.6 = (f32[8,128]{1,0:T(8,128)S(1)}, f32[8,128]{1,0:T(8,128)S(1)}, u32[]{:S(2)}, u32[]{:S(2)}) collective-permute-start(f32[8,128]{1,0:T(8,128)S(1)} %shard_map.187.s0), channel_id=1, source_target_pairs={{0,4},{2,6},{4,0},{6,2},{1,5},{3,7},{5,1},{7,3},{8,12},{10,14},{12... | collective-permute-start | bytes 12296 | tf_op jit(solution)/shard_map/ppermute | solution.py:430
  20.8 2.8 %collective-permute-start.5 = (f32[8,128]{1,0:T(8,128)S(1)}, f32[8,128]{1,0:T(8,128)S(1)}, u32[]{:S(2)}, u32[]{:S(2)}) collective-permute-start(f32[8,128]{1,0:T(8,128)S(1)} %shard_map.187.s0), channel_id=1, source_target_pairs={{0,6},{2,0},{4,2},{6,4},{1,7},{3,1},{5,3},{7,5},{8,14},{10,8},{12,... | collective-permute-start | bytes 12296 | tf_op jit(solution)/shard_map/ppermute | solution.py:430
  21.7 3.7 %collective-permute-start.4 = (f32[8,128]{1,0:T(8,128)S(1)}, f32[8,128]{1,0:T(8,128)S(1)}, u32[]{:S(2)}, u32[]{:S(2)}) collective-permute-start(f32[8,128]{1,0:T(8,128)S(1)} %shard_map.187.s0), channel_id=1, source_target_pairs={{0,2},{2,4},{4,6},{6,0},{1,3},{3,5},{5,7},{7,1},{8,10},{10,12},{12... | collective-permute-start | bytes 12296 | tf_op jit(solution)/shard_map/ppermute | solution.py:430
  27.7 26.6 %all-to-all-start = ((bf16[8,256,128]{2,1,0:T(8,128)(2,1)}), bf16[8,256,128]{2,1,0:T(8,128)(2,1)S(1)}, u32[]{:S(2)}, u32[]{:S(2)}) async-start(bf16[8,256,128]{2,1,0:T(8,128)(2,1)} %get-tuple-element.69), calls=%async_computation | async-start | bytes 1048576 | tf_op jit(solution)/shard_map/all_to_all | solution.py:487
  55.0 5.3 %collective-permute-start.10 = (bf16[1024,128]{1,0:T(8,128)(2,1)S(1)}, bf16[1024,128]{1,0:T(8,128)(2,1)S(1)}, u32[]{:S(2)}, u32[]{:S(2)}) collective-permute-start(bf16[1024,128]{1,0:T(8,128)(2,1)S(1)} %shard_map.190.a), channel_id=1, source_target_pairs={{0,24},{8,0},{16,8},{24,16},{1,25},{9,1},{17,9},{25,17},{2,26},{10... | collective-permute-start | bytes 786440 | tf_op jit(solution)/shard_map/ppermute | solution.py:430
  56.3 9.9 %collective-permute-start.9 = (bf16[1024,128]{1,0:T(8,128)(2,1)S(1)}, bf16[1024,128]{1,0:T(8,128)(2,1)S(1)}, u32[]{:S(2)}, u32[]{:S(2)}) collective-permute-start(bf16[1024,128]{1,0:T(8,128)(2,1)S(1)} %shard_map.190.a), channel_id=1, source_target_pairs={{0,8},{8,16},{16,24},{24,0},{1,9},{9,17},{17,25},{25,1},{2,10},{10... | collective-permute-start | bytes 786440 | tf_op jit(solution)/shard_map/ppermute | solution.py:430
  56.5 9.7 %collective-permute-start.8 = (bf16[1024,128]{1,0:T(8,128)(2,1)S(1)}, bf16[1024,128]{1,0:T(8,128)(2,1)S(1)}, u32[]{:S(2)}, u32[]{:S(2)}) collective-permute-start(bf16[1024,128]{1,0:T(8,128)(2,1)S(1)} %shard_map.190.a), channel_id=1, source_target_pairs={{0,16},{8,24},{16,0},{24,8},{1,17},{9,25},{17,1},{25,9},{2,18},{10... | collective-permute-start | bytes 786440 | tf_op jit(solution)/shard_map/ppermute | solution.py:430
  66.8 8.2 %collective-permute-start.14 = (bf16[4,1024,128]{2,1,0:T(8,128)(2,1)S(1)}, bf16[4,1024,128]{2,1,0:T(8,128)(2,1)S(1)}, u32[]{:S(2)}, u32[]{:S(2)}) collective-permute-start(bf16[4,1024,128]{2,1,0:T(8,128)(2,1)S(1)} %get-tuple-element.76.mine), channel_id=1, source_target_pairs={{0,1},{1,0},{2,3},{3,2},{4,5},{5,4},{6,7},{7,6},{8,9},{9,8},{10,11... | collective-permute-start | bytes 3145736 | tf_op jit(solution)/shard_map/ppermute | solution.py:430
  81.2 8.5 %collective-permute-start.16 = (bf16[4112,128]{1,0:T(8,128)(2,1)S(1)}, bf16[4112,128]{1,0:T(8,128)(2,1)S(1)}, u32[]{:S(2)}, u32[]{:S(2)}) collective-permute-start(bf16[4112,128]{1,0:T(8,128)(2,1)S(1)} %get-tuple-element.80), channel_id=1, source_target_pairs={{0,1},{1,0},{2,3},{3,2},{4,5},{5,4},{6,7},{7,6},{8,9},{9,8},{10,11... | collective-permute-start | bytes 3158024 | tf_op jit(solution)/shard_map/ppermute | solution.py:430
  81.6 7.6 %collective-permute-start.11 = (bf16[8,48,128]{2,1,0:T(8,128)(2,1)S(1)}, bf16[8,48,128]{2,1,0:T(8,128)(2,1)S(1)}, u32[]{:S(2)}, u32[]{:S(2)}) collective-permute-start(bf16[8,48,128]{2,1,0:T(8,128)(2,1)S(1)} %get-tuple-element.73), channel_id=1, source_target_pairs={{0,8},{8,16},{16,24},{24,0},{1,9},{9,17},{17,25},{25,1},{2,10},{10... | collective-permute-start | bytes 294920 | tf_op jit(solution)/shard_map/ppermute | solution.py:430
  81.7 7.6 %collective-permute-start.12 = (bf16[8,48,128]{2,1,0:T(8,128)(2,1)S(1)}, bf16[8,48,128]{2,1,0:T(8,128)(2,1)S(1)}, u32[]{:S(2)}, u32[]{:S(2)}) collective-permute-start(bf16[8,48,128]{2,1,0:T(8,128)(2,1)S(1)} %get-tuple-element.74), channel_id=1, source_target_pairs={{0,16},{8,24},{16,0},{24,8},{1,17},{9,25},{17,1},{25,9},{2,18},{10... | collective-permute-start | bytes 294920 | tf_op jit(solution)/shard_map/ppermute | solution.py:430
  83.4 6.2 %collective-permute-start.13 = (bf16[8,48,128]{2,1,0:T(8,128)(2,1)S(1)}, bf16[8,48,128]{2,1,0:T(8,128)(2,1)S(1)}, u32[]{:S(2)}, u32[]{:S(2)}) collective-permute-start(bf16[8,48,128]{2,1,0:T(8,128)(2,1)S(1)} %get-tuple-element.75), channel_id=1, source_target_pairs={{0,24},{8,0},{16,8},{24,16},{1,25},{9,1},{17,9},{25,17},{2,26},{10... | collective-permute-start | bytes 294920 | tf_op jit(solution)/shard_map/ppermute | solution.py:430
  89.6 3.6 %collective-permute-start.15 = (bf16[8,48,128]{2,1,0:T(8,128)(2,1)S(1)}, bf16[8,48,128]{2,1,0:T(8,128)(2,1)S(1)}, u32[]{:S(2)}, u32[]{:S(2)}) collective-permute-start(bf16[8,48,128]{2,1,0:T(8,128)(2,1)S(1)} %get-tuple-element.78.a), channel_id=1, source_target_pairs={{0,32},{32,0},{64,96},{96,64},{128,160},{160,128},{192,224},{224,1... | collective-permute-start | bytes 294920 | tf_op jit(solution)/shard_map/ppermute | solution.py:434
  93.7 5.1 %collective-permute-start.17 = (bf16[8,48,128]{2,1,0:T(8,128)(2,1)S(1)}, bf16[8,48,128]{2,1,0:T(8,128)(2,1)S(1)}, u32[]{:S(2)}, u32[]{:S(2)}) collective-permute-start(bf16[8,48,128]{2,1,0:T(8,128)(2,1)S(1)} %get-tuple-element.83.a), channel_id=1, source_target_pairs={{0,64},{32,96},{64,0},{96,32},{128,192},{160,224},{192,128},{224,1... | collective-permute-start | bytes 294920 | tf_op jit(solution)/shard_map/ppermute | solution.py:434
  94.3 12.6 %collective-permute-start.22 = (bf16[1040,128]{1,0:T(8,128)(2,1)S(1)}, bf16[1040,128]{1,0:T(8,128)(2,1)S(1)}, u32[]{:S(2)}, u32[]{:S(2)}) collective-permute-start(bf16[1040,128]{1,0:T(8,128)(2,1)S(1)} %get-tuple-element.89), channel_id=1, source_target_pairs={{0,8},{8,16},{16,24},{24,0},{1,9},{9,17},{17,25},{25,1},{2,10},{10... | collective-permute-start | bytes 798728 | tf_op jit(solution)/shard_map/ppermute | solution.py:430
  94.6 12.3 %collective-permute-start.23 = (bf16[1040,128]{1,0:T(8,128)(2,1)S(1)}, bf16[1040,128]{1,0:T(8,128)(2,1)S(1)}, u32[]{:S(2)}, u32[]{:S(2)}) collective-permute-start(bf16[1040,128]{1,0:T(8,128)(2,1)S(1)} %get-tuple-element.90), channel_id=1, source_target_pairs={{0,24},{8,0},{16,8},{24,16},{1,25},{9,1},{17,9},{25,17},{2,26},{10... | collective-permute-start | bytes 798728 | tf_op jit(solution)/shard_map/ppermute | solution.py:430
  96.9 11.0 %collective-permute-start.24 = (bf16[1040,128]{1,0:T(8,128)(2,1)S(1)}, bf16[1040,128]{1,0:T(8,128)(2,1)S(1)}, u32[]{:S(2)}, u32[]{:S(2)}) collective-permute-start(bf16[1040,128]{1,0:T(8,128)(2,1)S(1)} %get-tuple-element.91), channel_id=1, source_target_pairs={{0,16},{8,24},{16,0},{24,8},{1,17},{9,25},{17,1},{25,9},{2,18},{10... | collective-permute-start | bytes 798728 | tf_op jit(solution)/shard_map/ppermute | solution.py:430
  99.5 7.4 %collective-permute-start.18 = (bf16[8,48,128]{2,1,0:T(8,128)(2,1)S(1)}, bf16[8,48,128]{2,1,0:T(8,128)(2,1)S(1)}, u32[]{:S(2)}, u32[]{:S(2)}) collective-permute-start(bf16[8,48,128]{2,1,0:T(8,128)(2,1)S(1)} %get-tuple-element.84.a), channel_id=1, source_target_pairs={{0,128},{32,160},{64,192},{96,224},{128,0},{160,32},{192,64},{224,... | collective-permute-start | bytes 294920 | tf_op jit(solution)/shard_map/ppermute | solution.py:434
  108.9 16.9 %all-to-all-start.1 = ((bf16[8,272,128]{2,1,0:T(8,128)(2,1)}), bf16[8,272,128]{2,1,0:T(8,128)(2,1)S(1)}, u32[]{:S(2)}, u32[]{:S(2)}) async-start(bf16[8,272,128]{2,1,0:T(8,128)(2,1)} %get-tuple-element.94), calls=%async_computation.1 | async-start | bytes 1114112 | tf_op jit(solution)/shard_map/all_to_all | solution.py:573
  113.9 5.1 %collective-permute-start.21 = (bf16[8,48,128]{2,1,0:T(8,128)(2,1)S(1)}, bf16[8,48,128]{2,1,0:T(8,128)(2,1)S(1)}, u32[]{:S(2)}, u32[]{:S(2)}) collective-permute-start(bf16[8,48,128]{2,1,0:T(8,128)(2,1)S(1)} %get-tuple-element.85.p0), channel_id=1, source_target_pairs={{0,16},{8,24},{16,0},{24,8},{1,17},{9,25},{17,1},{25,9},{2,18},{10... | collective-permute-start | bytes 294920 | tf_op jit(solution)/shard_map/ppermute | solution.py:430
  114.6 5.0 %collective-permute-start.20 = (bf16[8,48,128]{2,1,0:T(8,128)(2,1)S(1)}, bf16[8,48,128]{2,1,0:T(8,128)(2,1)S(1)}, u32[]{:S(2)}, u32[]{:S(2)}) collective-permute-start(bf16[8,48,128]{2,1,0:T(8,128)(2,1)S(1)} %get-tuple-element.85.p0), channel_id=1, source_target_pairs={{0,24},{8,0},{16,8},{24,16},{1,25},{9,1},{17,9},{25,17},{2,26},{10... | collective-permute-start | bytes 294920 | tf_op jit(solution)/shard_map/ppermute | solution.py:430
  116.0 4.7 %collective-permute-start.19 = (bf16[8,48,128]{2,1,0:T(8,128)(2,1)S(1)}, bf16[8,48,128]{2,1,0:T(8,128)(2,1)S(1)}, u32[]{:S(2)}, u32[]{:S(2)}) collective-permute-start(bf16[8,48,128]{2,1,0:T(8,128)(2,1)S(1)} %get-tuple-element.85.p0), channel_id=1, source_target_pairs={{0,8},{8,16},{16,24},{24,0},{1,9},{9,17},{17,25},{25,1},{2,10},{10... | collective-permute-start | bytes 294920 | tf_op jit(solution)/shard_map/ppermute | solution.py:430
  116.5 14.0 %collective-permute-start.7 = (bf16[3,16,1024]{2,1,0:T(8,128)(2,1)S(1)}, bf16[3,16,1024]{2,1,0:T(8,128)(2,1)S(1)}, u32[]{:S(2)}, u32[]{:S(2)}) collective-permute-start(bf16[3,16,1024]{2,1,0:T(8,128)(2,1)S(1)} %copy-done.14), channel_id=1, source_target_pairs={{8,0},{16,8},{24,16},{32,24},{40,32},{48,40},{56,48},{64,56},{72,6... | collective-permute-start | bytes 294920 | tf_op jit(solution)/shard_map/ppermute | solution.py:439
  127.1 4.3 %collective-permute-start.27 = (f32[8,128]{1,0:T(8,128)S(1)}, f32[8,128]{1,0:T(8,128)S(1)}, u32[]{:S(2)}, u32[]{:S(2)}) collective-permute-start(f32[8,128]{1,0:T(8,128)S(1)} %get-tuple-element.97.p0), channel_id=1, source_target_pairs={{0,4},{2,6},{4,0},{6,2},{1,5},{3,7},{5,1},{7,3},{8,12},{10,14},{12... | collective-permute-start | bytes 12296 | tf_op jit(solution)/shard_map/ppermute | solution.py:430
  128.9 2.8 %collective-permute-start.26 = (f32[8,128]{1,0:T(8,128)S(1)}, f32[8,128]{1,0:T(8,128)S(1)}, u32[]{:S(2)}, u32[]{:S(2)}) collective-permute-start(f32[8,128]{1,0:T(8,128)S(1)} %get-tuple-element.97.p0), channel_id=1, source_target_pairs={{0,6},{2,0},{4,2},{6,4},{1,7},{3,1},{5,3},{7,5},{8,14},{10,8},{12,... | collective-permute-start | bytes 12296 | tf_op jit(solution)/shard_map/ppermute | solution.py:430
  129.7 3.7 %collective-permute-start.25 = (f32[8,128]{1,0:T(8,128)S(1)}, f32[8,128]{1,0:T(8,128)S(1)}, u32[]{:S(2)}, u32[]{:S(2)}) collective-permute-start(f32[8,128]{1,0:T(8,128)S(1)} %get-tuple-element.97.p0), channel_id=1, source_target_pairs={{0,2},{2,4},{4,6},{6,0},{1,3},{3,5},{5,7},{7,1},{8,10},{10,12},{12... | collective-permute-start | bytes 12296 | tf_op jit(solution)/shard_map/ppermute | solution.py:430
  134.2 10.1 %collective-permute-start.28 = (bf16[4,64,512]{2,1,0:T(8,128)(2,1)S(1)}, bf16[4,64,512]{2,1,0:T(8,128)(2,1)S(1)}, u32[]{:S(2)}, u32[]{:S(2)}) collective-permute-start(bf16[4,64,512]{2,1,0:T(8,128)(2,1)S(1)} %get-tuple-element.99), channel_id=1, source_target_pairs={{0,1},{1,0},{2,3},{3,2},{4,5},{5,4},{6,7},{7,6},{8,9},{9,8},{10,11... | collective-permute-start | bytes 786440 | tf_op jit(solution)/shard_map/ppermute | solution.py:430
  (14 other events, 116.9 us)

commit v2 on v1

--- a/solution.py
+++ b/solution.py
@@ -511,7 +511,7 @@
         grid=grid,
         in_specs=[
             spec(3, 128), spec(272), spec(32), spec(256), spec(128),
-            spec(3, 7), spec(128), whole(2, 1280, 128), ANY,
+            spec(3, 7), spec(128), whole(2, 1280, 128), VM,
         ],
         out_specs=[
             spec(128), spec(3, 128), spec(3, 16), spec(3, 16), pl.BlockSpec((NX, 2, 48, 128), lambda i: (0, i, 0, 0)), VM,
@@ -521,7 +521,7 @@
     next_head = along(head, -1)
 
     kv = call(
-        keys_kernel, shape((NZ * 128, HD), BF16), in_specs=[VM, ANY], out_specs=VM, us=0.5
+        keys_kernel, shape((NZ * 128, HD), BF16), in_specs=[VM, VM], out_specs=VM, us=0.5
     )(blk, hyena_done)
     piece_shape = shape((NZ, 48, 128), BF16)
     ring, *parts = call(

time: 146 us -> 146 us (level)
  no operation moved by 1% of the time
where the time goes in v2:
time: 146 us
  starting transfers between devices  69.7 us (48%)
  waiting for transfers between devices  39.4 us (27%)
  Pallas kernels  31.6 us (22%)
  local copies, waits for them, and re-layouts  2.2 us (2%)
  other arithmetic  1.67 us (1%)
    ppermute x22, starting transfers between devices, rotate(): return lax.ppermute(x, axis, [(i, (i + by) % size) for i in range(size)])  36.3 us
    ppermute x22, waiting for transfers between devices, rotate(): return lax.ppermute(x, axis, [(i, (i + by) % size) for i in range(size)])  25.3 us
    ppermute x4, starting transfers between devices, along(): lax.ppermute(x, ('z', 'x'), [(i, i + by) for i in range(count) if 0 <= i...  12.5 us
    all_to_all x1, starting transfers between devices, local(): blk = lax.all_to_all(payload, 'z', 0, 0)  11.9 us
    pallas_call x1, Pallas kernels, local(): call(hyena_kernel, [shape((ROWS, channels), BF16), shape((3, ROWS, channe...  11.8 us
    ppermute x3, waiting for transfers between devices, flip(): return lax.ppermute(x, axis, [(i, i ^ by) for i in range(size)])  7.44 us
    pallas_call x1, Pallas kernels, local(): call(attention_kernel, [shape((4096, 128), F32), shape((8, 128), F32), sh...  6.13 us
    all_to_all x1, starting transfers between devices, local(): back = lax.all_to_all(outgoing, 'z', 0, 0)  4.94 us
  transfers between devices with their start and end apart: 31, of which 21 were waited for; matrix products, arithmetic and copies ran while one was open for 1% of the time, Pallas kernels for 11%

profile of v2, /device:TPU:1, one launch (start us, length us, event | category | flops | bytes accessed | tf_op | source)
XLA Modules:
  0.0 145.6 jit_solution(5105062323400170083)
XLA Ops:
  1.2 3.3 %shard_map.186 = (bf16[256,512]{1,0:T(8,128)(2,1)}, bf16[272,512]{1,0:T(8,128)(2,1)}, bf16[272,1024]{1,0:T(8,128)(2,1)}, bf16[256,1024]{1,0:T(8,128)(2,1)}, bf16[32,1024]{1,0:T(8,128)(2,1)}, /*index=5*/f32[8,128]{1,0:T(8,128)}) custom-call(s32[3]{0:T(128)} %pad_add_fusion.idx, bf16[128,512]{1,0:T(8,128)(2,1)} %keys.1, bf16[128,512]{1,0:T(8,128)(2,1)} %values.1, ...), custom_call_target="tpu_custom_call" | custom-call | flops 1100000000 | tf_op jit(solution)/shard_map/pallas_call | solution.py:461
  4.6 4.1 %collective-permute-start = (bf16[272,1024]{1,0:T(8,128)(2,1)}, bf16[272,1024]{1,0:T(8,128)(2,1)S(1)}, u32[]{:S(2)}, u32[]{:S(2)}) collective-permute-start(bf16[272,1024]{1,0:T(8,128)(2,1)} %get-tuple-element.58), channel_id=1, source_target_pairs={{0,8},{8,16},{16,24},{24,32},{32,40},{40,48},{48,56},{56,64},{64,7... | collective-permute-start | bytes 1671176 | tf_op jit(solution)/shard_map/ppermute | solution.py:439
  11.1 5.8 %collective-permute-start.1 = (bf16[32,1024]{1,0:T(8,128)(2,1)}, bf16[32,1024]{1,0:T(8,128)(2,1)S(1)}, u32[]{:S(2)}, u32[]{:S(2)}) collective-permute-start(bf16[32,1024]{1,0:T(8,128)(2,1)} %get-tuple-element.59), channel_id=1, source_target_pairs={{0,16},{8,24},{16,32},{24,40},{32,48},{40,56},{48,64},{56,72},{64,... | collective-permute-start | bytes 196616 | tf_op jit(solution)/shard_map/ppermute | solution.py:439
  17.8 3.0 %collective-permute-start.6 = (f32[8,128]{1,0:T(8,128)S(1)}, f32[8,128]{1,0:T(8,128)S(1)}, u32[]{:S(2)}, u32[]{:S(2)}) collective-permute-start(f32[8,128]{1,0:T(8,128)S(1)} %shard_map.187.s0), channel_id=1, source_target_pairs={{0,4},{2,6},{4,0},{6,2},{1,5},{3,7},{5,1},{7,3},{8,12},{10,14},{12... | collective-permute-start | bytes 12296 | tf_op jit(solution)/shard_map/ppermute | solution.py:430
  21.7 1.3 collective-permute-start.4
  23.5 1.9 %collective-permute-done.4.s1 = f32[8,128]{1,0:T(8,128)S(1)} collective-permute-done((f32[8,128]{1,0:T(8,128)S(1)}, f32[8,128]{1,0:T(8,128)S(1)}, u32[]{:S(2)}, u32[]{:S(2)}) %collective-permute-start.4) | collective-permute-done | bytes 4128 | tf_op jit(solution)/shard_map/ppermute | solution.py:430
  25.5 1.6 %shard_map.188 = (bf16[8,256,128]{2,1,0:T(8,128)(2,1)}, f32[8,128]{1,0:T(8,128)S(1)}, f32[8,128]{1,0:T(8,128)S(1)}) custom-call(s32[3]{0:T(128)S(1)} %copy-done, bf16[256,512]{1,0:T(8,128)(2,1)S(1)} %copy-done.7, bf16[272,512]{1,0:T(8,128)(2,1)S(1)} %collective-permute-done.3.other, f32[1,512]{1,0:T(1,128)S(1)} %bitcast.25, f32[1,512]{1,0:T(1,128)S(1)} %bitcast.29, ...), custom_call_target="tpu_custom_call" | custom-call | flops 1650000000 | tf_op jit(solution)/shard_map/pallas_call | solution.py:480
  27.7 11.9 %all-to-all-start = ((bf16[8,256,128]{2,1,0:T(8,128)(2,1)}), bf16[8,256,128]{2,1,0:T(8,128)(2,1)S(1)}, u32[]{:S(2)}, u32[]{:S(2)}) async-start(bf16[8,256,128]{2,1,0:T(8,128)(2,1)} %get-tuple-element.69), calls=%async_computation | async-start | bytes 1048576 | tf_op jit(solution)/shard_map/all_to_all | solution.py:487
  39.6 11.8 %shard_map.189 = (bf16[128,1024]{1,0:T(8,128)(2,1)}, bf16[3,128,1024]{2,1,0:T(8,128)(2,1)}, bf16[3,16,1024]{2,1,0:T(8,128)(2,1)}, f32[3,16,1024]{2,1,0:T(8,128)}...) custom-call(bf16[3,128,1024]{2,1,0:T(8,128)(2,1)} %bitcast.35, bf16[272,1024]{1,0:T(8,128)(2,1)} %copy-done.1, ...), custom_call_target="tpu_custom_call" | custom-call | flops 12099999744 | tf_op jit(solution)/shard_map/pallas_call | solution.py:500
  51.4 2.8 %all-to-all-done.blk = bf16[8,256,128]{2,1,0:T(8,128)(2,1)S(1)} async-done(((bf16[8,256,128]{2,1,0:T(8,128)(2,1)}), bf16[8,256,128]{2,1,0:T(8,128)(2,1)S(1)}, u32[]{:S(2)}, u32[]{:S(2)}) %all-to-all-start) | async-done | bytes 524320 | tf_op jit(solution)/shard_map/all_to_all | solution.py:487
  55.0 1.4 collective-permute-start.10
  57.6 2.7 %collective-permute-done.10.d = bf16[1024,128]{1,0:T(8,128)(2,1)S(1)} collective-permute-done((bf16[1024,128]{1,0:T(8,128)(2,1)S(1)}, bf16[1024,128]{1,0:T(8,128)(2,1)S(1)}, u32[]{:S(2)}, u32[]{:S(2)}) %collective-permute-start.10) | collective-permute-done | bytes 262176 | tf_op jit(solution)/shard_map/ppermute | solution.py:430
  60.3 5.9 %collective-permute-done.9.b = bf16[1024,128]{1,0:T(8,128)(2,1)S(1)} collective-permute-done((bf16[1024,128]{1,0:T(8,128)(2,1)S(1)}, bf16[1024,128]{1,0:T(8,128)(2,1)S(1)}, u32[]{:S(2)}, u32[]{:S(2)}) %collective-permute-start.9) | collective-permute-done | bytes 262176 | tf_op jit(solution)/shard_map/ppermute | solution.py:430
  66.8 6.0 %collective-permute-start.14 = (bf16[4,1024,128]{2,1,0:T(8,128)(2,1)S(1)}, bf16[4,1024,128]{2,1,0:T(8,128)(2,1)S(1)}, u32[]{:S(2)}, u32[]{:S(2)}) collective-permute-start(bf16[4,1024,128]{2,1,0:T(8,128)(2,1)S(1)} %get-tuple-element.76.mine), channel_id=1, source_target_pairs={{0,1},{1,0},{2,3},{3,2},{4,5},{5,4},{6,7},{7,6},{8,9},{9,8},{10,11... | collective-permute-start | bytes 3145736 | tf_op jit(solution)/shard_map/ppermute | solution.py:430
  72.8 2.3 %collective-permute-done.14.pair = bf16[4,1024,128]{2,1,0:T(8,128)(2,1)S(1)} collective-permute-done((bf16[4,1024,128]{2,1,0:T(8,128)(2,1)S(1)}, bf16[4,1024,128]{2,1,0:T(8,128)(2,1)S(1)}, u32[]{:S(2)}, u32[]{:S(2)}) %collective-permute-start.14) | collective-permute-done | bytes 1048608 | tf_op jit(solution)/shard_map/ppermute | solution.py:430
  75.1 6.1 %shard_map.192 = (f32[4096,128]{1,0:T(8,128)S(1)}, f32[8,128]{1,0:T(8,128)S(1)}, bf16[4112,128]{1,0:T(8,128)(2,1)S(1)}, bf16[8,128,128]{2,1,0:T(8,128)(2,1)S(1)}) custom-call(s32[3]{0:T(128)S(1)} %copy-done, bf16[8,256,128]{2,1,0:T(8,128)(2,1)S(1)} %all-to-all-done.blk, bf16[4,1024,128]{2,1,0:T(8,128)(2,1)S(1)} %get-tuple-element.76.mine, ...), custom_call_target="tpu_custom_call" | custom-call | flops 7699999744 | tf_op jit(solution)/shard_map/pallas_call | solution.py:535
  81.7 1.7 %collective-permute-start.12 = (bf16[8,48,128]{2,1,0:T(8,128)(2,1)S(1)}, bf16[8,48,128]{2,1,0:T(8,128)(2,1)S(1)}, u32[]{:S(2)}, u32[]{:S(2)}) collective-permute-start(bf16[8,48,128]{2,1,0:T(8,128)(2,1)S(1)} %get-tuple-element.74), channel_id=1, source_target_pairs={{0,16},{8,24},{16,0},{24,8},{1,17},{9,25},{17,1},{25,9},{2,18},{10... | collective-permute-start | bytes 294920 | tf_op jit(solution)/shard_map/ppermute | solution.py:430
  84.3 4.9 %collective-permute-done.11.p1 = bf16[8,48,128]{2,1,0:T(8,128)(2,1)S(1)} collective-permute-done((bf16[8,48,128]{2,1,0:T(8,128)(2,1)S(1)}, bf16[8,48,128]{2,1,0:T(8,128)(2,1)S(1)}, u32[]{:S(2)}, u32[]{:S(2)}) %collective-permute-start.11) | collective-permute-done | bytes 98336 | tf_op jit(solution)/shard_map/ppermute | solution.py:430
  90.4 2.7 %collective-permute-done.15.b = bf16[8,48,128]{2,1,0:T(8,128)(2,1)S(1)} collective-permute-done((bf16[8,48,128]{2,1,0:T(8,128)(2,1)S(1)}, bf16[8,48,128]{2,1,0:T(8,128)(2,1)S(1)}, u32[]{:S(2)}, u32[]{:S(2)}) %collective-permute-start.15) | collective-permute-done | bytes 98336 | tf_op jit(solution)/shard_map/ppermute | solution.py:434
  94.6 2.4 %collective-permute-start.23 = (bf16[1040,128]{1,0:T(8,128)(2,1)S(1)}, bf16[1040,128]{1,0:T(8,128)(2,1)S(1)}, u32[]{:S(2)}, u32[]{:S(2)}) collective-permute-start(bf16[1040,128]{1,0:T(8,128)(2,1)S(1)} %get-tuple-element.90), channel_id=1, source_target_pairs={{0,24},{8,0},{16,8},{24,16},{1,25},{9,1},{17,9},{25,17},{2,26},{10... | collective-permute-start | bytes 798728 | tf_op jit(solution)/shard_map/ppermute | solution.py:430
  99.5 3.5 %collective-permute-start.18 = (bf16[8,48,128]{2,1,0:T(8,128)(2,1)S(1)}, bf16[8,48,128]{2,1,0:T(8,128)(2,1)S(1)}, u32[]{:S(2)}, u32[]{:S(2)}) collective-permute-start(bf16[8,48,128]{2,1,0:T(8,128)(2,1)S(1)} %get-tuple-element.84.a), channel_id=1, source_target_pairs={{0,128},{32,160},{64,192},{96,224},{128,0},{160,32},{192,64},{224,... | collective-permute-start | bytes 294920 | tf_op jit(solution)/shard_map/ppermute | solution.py:434
  103.0 3.8 %collective-permute-done.18.b = bf16[8,48,128]{2,1,0:T(8,128)(2,1)S(1)} collective-permute-done((bf16[8,48,128]{2,1,0:T(8,128)(2,1)S(1)}, bf16[8,48,128]{2,1,0:T(8,128)(2,1)S(1)}, u32[]{:S(2)}, u32[]{:S(2)}) %collective-permute-start.18) | collective-permute-done | bytes 98336 | tf_op jit(solution)/shard_map/ppermute | solution.py:434
  108.9 4.9 %all-to-all-start.1 = ((bf16[8,272,128]{2,1,0:T(8,128)(2,1)}), bf16[8,272,128]{2,1,0:T(8,128)(2,1)S(1)}, u32[]{:S(2)}, u32[]{:S(2)}) async-start(bf16[8,272,128]{2,1,0:T(8,128)(2,1)} %get-tuple-element.94), calls=%async_computation.1 | async-start | bytes 1114112 | tf_op jit(solution)/shard_map/all_to_all | solution.py:573
  114.6 1.5 %collective-permute-start.20 = (bf16[8,48,128]{2,1,0:T(8,128)(2,1)S(1)}, bf16[8,48,128]{2,1,0:T(8,128)(2,1)S(1)}, u32[]{:S(2)}, u32[]{:S(2)}) collective-permute-start(bf16[8,48,128]{2,1,0:T(8,128)(2,1)S(1)} %get-tuple-element.85.p0), channel_id=1, source_target_pairs={{0,24},{8,0},{16,8},{24,16},{1,25},{9,1},{17,9},{25,17},{2,26},{10... | collective-permute-start | bytes 294920 | tf_op jit(solution)/shard_map/ppermute | solution.py:430
  116.5 1.3 collective-permute-start.7
  120.7 1.5 %shard_map.198 = (f32[128,1024]{1,0:T(8,128)}, f32[3,7,1024]{2,1,0:T(8,128)}, f32[8,128]{1,0:T(8,128)S(1)}) custom-call(s32[3]{0:T(128)S(1)} %copy-done, bf16[8,48,128]{2,1,0:T(8,128)(2,1)S(1)} %get-tuple-element.85.p0, bf16[8,48,128]{2,1,0:T(8,128)(2,1)S(1)} %collective-permute-done.19.p1, bf16[8,48,128]{2,1,0:T(8,128)(2,1)S(1)} %collective-permute-done.20.p3, ...), custom_call_target="tpu_custom_call" | custom-call | flops 1100000000 | tf_op jit(solution)/shard_map/pallas_call | solution.py:576
  122.2 3.6 %all-to-all-done.1.back = bf16[8,272,128]{2,1,0:T(8,128)(2,1)S(1)} async-done(((bf16[8,272,128]{2,1,0:T(8,128)(2,1)}), bf16[8,272,128]{2,1,0:T(8,128)(2,1)S(1)}, u32[]{:S(2)}, u32[]{:S(2)}) %all-to-all-start.1) | async-done | bytes 557088 | tf_op jit(solution)/shard_map/all_to_all | solution.py:573
  125.8 1.3 shard_map.200
  127.2 1.8 %collective-permute-start.27 = (f32[8,128]{1,0:T(8,128)S(1)}, f32[8,128]{1,0:T(8,128)S(1)}, u32[]{:S(2)}, u32[]{:S(2)}) collective-permute-start(f32[8,128]{1,0:T(8,128)S(1)} %get-tuple-element.97.p0), channel_id=1, source_target_pairs={{0,4},{2,6},{4,0},{6,2},{1,5},{3,7},{5,1},{7,3},{8,12},{10,14},{12... | collective-permute-start | bytes 12296 | tf_op jit(solution)/shard_map/ppermute | solution.py:430
  131.7 1.7 %collective-permute-done.25.p1 = f32[8,128]{1,0:T(8,128)S(1)} collective-permute-done((f32[8,128]{1,0:T(8,128)S(1)}, f32[8,128]{1,0:T(8,128)S(1)}, u32[]{:S(2)}, u32[]{:S(2)}) %collective-permute-start.25) | collective-permute-done | bytes 4128 | tf_op jit(solution)/shard_map/ppermute | solution.py:430
  134.2 8.9 %collective-permute-start.28 = (bf16[4,64,512]{2,1,0:T(8,128)(2,1)S(1)}, bf16[4,64,512]{2,1,0:T(8,128)(2,1)S(1)}, u32[]{:S(2)}, u32[]{:S(2)}) collective-permute-start(bf16[4,64,512]{2,1,0:T(8,128)(2,1)S(1)} %get-tuple-element.99), channel_id=1, source_target_pairs={{0,1},{1,0},{2,3},{3,2},{4,5},{5,4},{6,7},{7,6},{8,9},{9,8},{10,11... | collective-permute-start | bytes 786440 | tf_op jit(solution)/shard_map/ppermute | solution.py:430
  144.3 1.4 shard_map.202
  (91 shorter events, 25.8 us)
Async XLA Ops:
  4.6 20.9 %copy-start = (s32[3]{0:T(128)S(1)}, s32[3]{0:T(128)}, u32[]{:S(2)}) copy-start(s32[3]{0:T(128)} %pad_add_fusion.idx) | copy-start | bytes 40
  4.6 20.8 %collective-permute-start = (bf16[272,1024]{1,0:T(8,128)(2,1)}, bf16[272,1024]{1,0:T(8,128)(2,1)S(1)}, u32[]{:S(2)}, u32[]{:S(2)}) collective-permute-start(bf16[272,1024]{1,0:T(8,128)(2,1)} %get-tuple-element.58), channel_id=1, source_target_pairs={{0,8},{8,16},{16,24},{24,32},{32,40},{40,48},{48,56},{56,64},{64,7... | collective-permute-start | bytes 1671176 | tf_op jit(solution)/shard_map/ppermute | solution.py:439
  8.8 16.7 %collective-permute-start.2 = (bf16[256,1024]{1,0:T(8,128)(2,1)}, bf16[256,1024]{1,0:T(8,128)(2,1)S(1)}, u32[]{:S(2)}, u32[]{:S(2)}) collective-permute-start(bf16[256,1024]{1,0:T(8,128)(2,1)} %get-tuple-element.60), channel_id=1, source_target_pairs={{8,0},{16,8},{24,16},{32,24},{40,32},{48,40},{56,48},{64,56},{72,6... | collective-permute-start | bytes 1572872 | tf_op jit(solution)/shard_map/ppermute | solution.py:439
  10.1 6.8 %collective-permute-start.3 = (bf16[272,512]{1,0:T(8,128)(2,1)}, bf16[272,512]{1,0:T(8,128)(2,1)S(1)}, u32[]{:S(2)}, u32[]{:S(2)}) collective-permute-start(bf16[272,512]{1,0:T(8,128)(2,1)} %get-tuple-element.62), channel_id=1, source_target_pairs={{0,1},{1,0},{2,3},{3,2},{4,5},{5,4},{6,7},{7,6},{8,9},{9,8},{10,11... | collective-permute-start | bytes 835592 | tf_op jit(solution)/shard_map/ppermute | solution.py:430
  11.1 10.6 %collective-permute-start.1 = (bf16[32,1024]{1,0:T(8,128)(2,1)}, bf16[32,1024]{1,0:T(8,128)(2,1)S(1)}, u32[]{:S(2)}, u32[]{:S(2)}) collective-permute-start(bf16[32,1024]{1,0:T(8,128)(2,1)} %get-tuple-element.59), channel_id=1, source_target_pairs={{0,16},{8,24},{16,32},{24,40},{32,48},{40,56},{48,64},{56,72},{64,... | collective-permute-start | bytes 196616 | tf_op jit(solution)/shard_map/ppermute | solution.py:439
  17.8 5.2 %collective-permute-start.6 = (f32[8,128]{1,0:T(8,128)S(1)}, f32[8,128]{1,0:T(8,128)S(1)}, u32[]{:S(2)}, u32[]{:S(2)}) collective-permute-start(f32[8,128]{1,0:T(8,128)S(1)} %shard_map.187.s0), channel_id=1, source_target_pairs={{0,4},{2,6},{4,0},{6,2},{1,5},{3,7},{5,1},{7,3},{8,12},{10,14},{12... | collective-permute-start | bytes 12296 | tf_op jit(solution)/shard_map/ppermute | solution.py:430
  20.8 2.8 %collective-permute-start.5 = (f32[8,128]{1,0:T(8,128)S(1)}, f32[8,128]{1,0:T(8,128)S(1)}, u32[]{:S(2)}, u32[]{:S(2)}) collective-permute-start(f32[8,128]{1,0:T(8,128)S(1)} %shard_map.187.s0), channel_id=1, source_target_pairs={{0,6},{2,0},{4,2},{6,4},{1,7},{3,1},{5,3},{7,5},{8,14},{10,8},{12,... | collective-permute-start | bytes 12296 | tf_op jit(solution)/shard_map/ppermute | solution.py:430
  21.7 3.7 %collective-permute-start.4 = (f32[8,128]{1,0:T(8,128)S(1)}, f32[8,128]{1,0:T(8,128)S(1)}, u32[]{:S(2)}, u32[]{:S(2)}) collective-permute-start(f32[8,128]{1,0:T(8,128)S(1)} %shard_map.187.s0), channel_id=1, source_target_pairs={{0,2},{2,4},{4,6},{6,0},{1,3},{3,5},{5,7},{7,1},{8,10},{10,12},{12... | collective-permute-start | bytes 12296 | tf_op jit(solution)/shard_map/ppermute | solution.py:430
  27.7 26.6 %all-to-all-start = ((bf16[8,256,128]{2,1,0:T(8,128)(2,1)}), bf16[8,256,128]{2,1,0:T(8,128)(2,1)S(1)}, u32[]{:S(2)}, u32[]{:S(2)}) async-start(bf16[8,256,128]{2,1,0:T(8,128)(2,1)} %get-tuple-element.69), calls=%async_computation | async-start | bytes 1048576 | tf_op jit(solution)/shard_map/all_to_all | solution.py:487
  55.0 5.3 %collective-permute-start.10 = (bf16[1024,128]{1,0:T(8,128)(2,1)S(1)}, bf16[1024,128]{1,0:T(8,128)(2,1)S(1)}, u32[]{:S(2)}, u32[]{:S(2)}) collective-permute-start(bf16[1024,128]{1,0:T(8,128)(2,1)S(1)} %shard_map.190.a), channel_id=1, source_target_pairs={{0,24},{8,0},{16,8},{24,16},{1,25},{9,1},{17,9},{25,17},{2,26},{10... | collective-permute-start | bytes 786440 | tf_op jit(solution)/shard_map/ppermute | solution.py:430
  56.3 9.9 %collective-permute-start.9 = (bf16[1024,128]{1,0:T(8,128)(2,1)S(1)}, bf16[1024,128]{1,0:T(8,128)(2,1)S(1)}, u32[]{:S(2)}, u32[]{:S(2)}) collective-permute-start(bf16[1024,128]{1,0:T(8,128)(2,1)S(1)} %shard_map.190.a), channel_id=1, source_target_pairs={{0,8},{8,16},{16,24},{24,0},{1,9},{9,17},{17,25},{25,1},{2,10},{10... | collective-permute-start | bytes 786440 | tf_op jit(solution)/shard_map/ppermute | solution.py:430
  56.5 9.7 %collective-permute-start.8 = (bf16[1024,128]{1,0:T(8,128)(2,1)S(1)}, bf16[1024,128]{1,0:T(8,128)(2,1)S(1)}, u32[]{:S(2)}, u32[]{:S(2)}) collective-permute-start(bf16[1024,128]{1,0:T(8,128)(2,1)S(1)} %shard_map.190.a), channel_id=1, source_target_pairs={{0,16},{8,24},{16,0},{24,8},{1,17},{9,25},{17,1},{25,9},{2,18},{10... | collective-permute-start | bytes 786440 | tf_op jit(solution)/shard_map/ppermute | solution.py:430
  66.8 8.2 %collective-permute-start.14 = (bf16[4,1024,128]{2,1,0:T(8,128)(2,1)S(1)}, bf16[4,1024,128]{2,1,0:T(8,128)(2,1)S(1)}, u32[]{:S(2)}, u32[]{:S(2)}) collective-permute-start(bf16[4,1024,128]{2,1,0:T(8,128)(2,1)S(1)} %get-tuple-element.76.mine), channel_id=1, source_target_pairs={{0,1},{1,0},{2,3},{3,2},{4,5},{5,4},{6,7},{7,6},{8,9},{9,8},{10,11... | collective-permute-start | bytes 3145736 | tf_op jit(solution)/shard_map/ppermute | solution.py:430
  81.2 8.5 %collective-permute-start.16 = (bf16[4112,128]{1,0:T(8,128)(2,1)S(1)}, bf16[4112,128]{1,0:T(8,128)(2,1)S(1)}, u32[]{:S(2)}, u32[]{:S(2)}) collective-permute-start(bf16[4112,128]{1,0:T(8,128)(2,1)S(1)} %get-tuple-element.80), channel_id=1, source_target_pairs={{0,1},{1,0},{2,3},{3,2},{4,5},{5,4},{6,7},{7,6},{8,9},{9,8},{10,11... | collective-permute-start | bytes 3158024 | tf_op jit(solution)/shard_map/ppermute | solution.py:430
  81.6 7.6 %collective-permute-start.11 = (bf16[8,48,128]{2,1,0:T(8,128)(2,1)S(1)}, bf16[8,48,128]{2,1,0:T(8,128)(2,1)S(1)}, u32[]{:S(2)}, u32[]{:S(2)}) collective-permute-start(bf16[8,48,128]{2,1,0:T(8,128)(2,1)S(1)} %get-tuple-element.73), channel_id=1, source_target_pairs={{0,8},{8,16},{16,24},{24,0},{1,9},{9,17},{17,25},{25,1},{2,10},{10... | collective-permute-start | bytes 294920 | tf_op jit(solution)/shard_map/ppermute | solution.py:430
  81.7 7.6 %collective-permute-start.12 = (bf16[8,48,128]{2,1,0:T(8,128)(2,1)S(1)}, bf16[8,48,128]{2,1,0:T(8,128)(2,1)S(1)}, u32[]{:S(2)}, u32[]{:S(2)}) collective-permute-start(bf16[8,48,128]{2,1,0:T(8,128)(2,1)S(1)} %get-tuple-element.74), channel_id=1, source_target_pairs={{0,16},{8,24},{16,0},{24,8},{1,17},{9,25},{17,1},{25,9},{2,18},{10... | collective-permute-start | bytes 294920 | tf_op jit(solution)/shard_map/ppermute | solution.py:430
  83.4 6.2 %collective-permute-start.13 = (bf16[8,48,128]{2,1,0:T(8,128)(2,1)S(1)}, bf16[8,48,128]{2,1,0:T(8,128)(2,1)S(1)}, u32[]{:S(2)}, u32[]{:S(2)}) collective-permute-start(bf16[8,48,128]{2,1,0:T(8,128)(2,1)S(1)} %get-tuple-element.75), channel_id=1, source_target_pairs={{0,24},{8,0},{16,8},{24,16},{1,25},{9,1},{17,9},{25,17},{2,26},{10... | collective-permute-start | bytes 294920 | tf_op jit(solution)/shard_map/ppermute | solution.py:430
  89.6 3.6 %collective-permute-start.15 = (bf16[8,48,128]{2,1,0:T(8,128)(2,1)S(1)}, bf16[8,48,128]{2,1,0:T(8,128)(2,1)S(1)}, u32[]{:S(2)}, u32[]{:S(2)}) collective-permute-start(bf16[8,48,128]{2,1,0:T(8,128)(2,1)S(1)} %get-tuple-element.78.a), channel_id=1, source_target_pairs={{0,32},{32,0},{64,96},{96,64},{128,160},{160,128},{192,224},{224,1... | collective-permute-start | bytes 294920 | tf_op jit(solution)/shard_map/ppermute | solution.py:434
  93.7 5.1 %collective-permute-start.17 = (bf16[8,48,128]{2,1,0:T(8,128)(2,1)S(1)}, bf16[8,48,128]{2,1,0:T(8,128)(2,1)S(1)}, u32[]{:S(2)}, u32[]{:S(2)}) collective-permute-start(bf16[8,48,128]{2,1,0:T(8,128)(2,1)S(1)} %get-tuple-element.83.a), channel_id=1, source_target_pairs={{0,64},{32,96},{64,0},{96,32},{128,192},{160,224},{192,128},{224,1... | collective-permute-start | bytes 294920 | tf_op jit(solution)/shard_map/ppermute | solution.py:434
  94.3 12.6 %collective-permute-start.22 = (bf16[1040,128]{1,0:T(8,128)(2,1)S(1)}, bf16[1040,128]{1,0:T(8,128)(2,1)S(1)}, u32[]{:S(2)}, u32[]{:S(2)}) collective-permute-start(bf16[1040,128]{1,0:T(8,128)(2,1)S(1)} %get-tuple-element.89), channel_id=1, source_target_pairs={{0,8},{8,16},{16,24},{24,0},{1,9},{9,17},{17,25},{25,1},{2,10},{10... | collective-permute-start | bytes 798728 | tf_op jit(solution)/shard_map/ppermute | solution.py:430
  94.6 12.3 %collective-permute-start.23 = (bf16[1040,128]{1,0:T(8,128)(2,1)S(1)}, bf16[1040,128]{1,0:T(8,128)(2,1)S(1)}, u32[]{:S(2)}, u32[]{:S(2)}) collective-permute-start(bf16[1040,128]{1,0:T(8,128)(2,1)S(1)} %get-tuple-element.90), channel_id=1, source_target_pairs={{0,24},{8,0},{16,8},{24,16},{1,25},{9,1},{17,9},{25,17},{2,26},{10... | collective-permute-start | bytes 798728 | tf_op jit(solution)/shard_map/ppermute | solution.py:430
  96.9 11.0 %collective-permute-start.24 = (bf16[1040,128]{1,0:T(8,128)(2,1)S(1)}, bf16[1040,128]{1,0:T(8,128)(2,1)S(1)}, u32[]{:S(2)}, u32[]{:S(2)}) collective-permute-start(bf16[1040,128]{1,0:T(8,128)(2,1)S(1)} %get-tuple-element.91), channel_id=1, source_target_pairs={{0,16},{8,24},{16,0},{24,8},{1,17},{9,25},{17,1},{25,9},{2,18},{10... | collective-permute-start | bytes 798728 | tf_op jit(solution)/shard_map/ppermute | solution.py:430
  99.5 7.4 %collective-permute-start.18 = (bf16[8,48,128]{2,1,0:T(8,128)(2,1)S(1)}, bf16[8,48,128]{2,1,0:T(8,128)(2,1)S(1)}, u32[]{:S(2)}, u32[]{:S(2)}) collective-permute-start(bf16[8,48,128]{2,1,0:T(8,128)(2,1)S(1)} %get-tuple-element.84.a), channel_id=1, source_target_pairs={{0,128},{32,160},{64,192},{96,224},{128,0},{160,32},{192,64},{224,... | collective-permute-start | bytes 294920 | tf_op jit(solution)/shard_map/ppermute | solution.py:434
  108.9 17.0 %all-to-all-start.1 = ((bf16[8,272,128]{2,1,0:T(8,128)(2,1)}), bf16[8,272,128]{2,1,0:T(8,128)(2,1)S(1)}, u32[]{:S(2)}, u32[]{:S(2)}) async-start(bf16[8,272,128]{2,1,0:T(8,128)(2,1)} %get-tuple-element.94), calls=%async_computation.1 | async-start | bytes 1114112 | tf_op jit(solution)/shard_map/all_to_all | solution.py:573
  113.9 5.1 %collective-permute-start.21 = (bf16[8,48,128]{2,1,0:T(8,128)(2,1)S(1)}, bf16[8,48,128]{2,1,0:T(8,128)(2,1)S(1)}, u32[]{:S(2)}, u32[]{:S(2)}) collective-permute-start(bf16[8,48,128]{2,1,0:T(8,128)(2,1)S(1)} %get-tuple-element.85.p0), channel_id=1, source_target_pairs={{0,16},{8,24},{16,0},{24,8},{1,17},{9,25},{17,1},{25,9},{2,18},{10... | collective-permute-start | bytes 294920 | tf_op jit(solution)/shard_map/ppermute | solution.py:430
  114.6 5.0 %collective-permute-start.20 = (bf16[8,48,128]{2,1,0:T(8,128)(2,1)S(1)}, bf16[8,48,128]{2,1,0:T(8,128)(2,1)S(1)}, u32[]{:S(2)}, u32[]{:S(2)}) collective-permute-start(bf16[8,48,128]{2,1,0:T(8,128)(2,1)S(1)} %get-tuple-element.85.p0), channel_id=1, source_target_pairs={{0,24},{8,0},{16,8},{24,16},{1,25},{9,1},{17,9},{25,17},{2,26},{10... | collective-permute-start | bytes 294920 | tf_op jit(solution)/shard_map/ppermute | solution.py:430
  116.1 4.7 %collective-permute-start.19 = (bf16[8,48,128]{2,1,0:T(8,128)(2,1)S(1)}, bf16[8,48,128]{2,1,0:T(8,128)(2,1)S(1)}, u32[]{:S(2)}, u32[]{:S(2)}) collective-permute-start(bf16[8,48,128]{2,1,0:T(8,128)(2,1)S(1)} %get-tuple-element.85.p0), channel_id=1, source_target_pairs={{0,8},{8,16},{16,24},{24,0},{1,9},{9,17},{17,25},{25,1},{2,10},{10... | collective-permute-start | bytes 294920 | tf_op jit(solution)/shard_map/ppermute | solution.py:430
  116.5 14.0 %collective-permute-start.7 = (bf16[3,16,1024]{2,1,0:T(8,128)(2,1)S(1)}, bf16[3,16,1024]{2,1,0:T(8,128)(2,1)S(1)}, u32[]{:S(2)}, u32[]{:S(2)}) collective-permute-start(bf16[3,16,1024]{2,1,0:T(8,128)(2,1)S(1)} %copy-done.14), channel_id=1, source_target_pairs={{8,0},{16,8},{24,16},{32,24},{40,32},{48,40},{56,48},{64,56},{72,6... | collective-permute-start | bytes 294920 | tf_op jit(solution)/shard_map/ppermute | solution.py:439
  127.2 4.3 %collective-permute-start.27 = (f32[8,128]{1,0:T(8,128)S(1)}, f32[8,128]{1,0:T(8,128)S(1)}, u32[]{:S(2)}, u32[]{:S(2)}) collective-permute-start(f32[8,128]{1,0:T(8,128)S(1)} %get-tuple-element.97.p0), channel_id=1, source_target_pairs={{0,4},{2,6},{4,0},{6,2},{1,5},{3,7},{5,1},{7,3},{8,12},{10,14},{12... | collective-permute-start | bytes 12296 | tf_op jit(solution)/shard_map/ppermute | solution.py:430
  128.9 2.8 %collective-permute-start.26 = (f32[8,128]{1,0:T(8,128)S(1)}, f32[8,128]{1,0:T(8,128)S(1)}, u32[]{:S(2)}, u32[]{:S(2)}) collective-permute-start(f32[8,128]{1,0:T(8,128)S(1)} %get-tuple-element.97.p0), channel_id=1, source_target_pairs={{0,6},{2,0},{4,2},{6,4},{1,7},{3,1},{5,3},{7,5},{8,14},{10,8},{12,... | collective-permute-start | bytes 12296 | tf_op jit(solution)/shard_map/ppermute | solution.py:430
  129.7 3.7 %collective-permute-start.25 = (f32[8,128]{1,0:T(8,128)S(1)}, f32[8,128]{1,0:T(8,128)S(1)}, u32[]{:S(2)}, u32[]{:S(2)}) collective-permute-start(f32[8,128]{1,0:T(8,128)S(1)} %get-tuple-element.97.p0), channel_id=1, source_target_pairs={{0,2},{2,4},{4,6},{6,0},{1,3},{3,5},{5,7},{7,1},{8,10},{10,12},{12... | collective-permute-start | bytes 12296 | tf_op jit(solution)/shard_map/ppermute | solution.py:430
  134.2 10.1 %collective-permute-start.28 = (bf16[4,64,512]{2,1,0:T(8,128)(2,1)S(1)}, bf16[4,64,512]{2,1,0:T(8,128)(2,1)S(1)}, u32[]{:S(2)}, u32[]{:S(2)}) collective-permute-start(bf16[4,64,512]{2,1,0:T(8,128)(2,1)S(1)} %get-tuple-element.99), channel_id=1, source_target_pairs={{0,1},{1,0},{2,3},{3,2},{4,5},{5,4},{6,7},{7,6},{8,9},{9,8},{10,11... | collective-permute-start | bytes 786440 | tf_op jit(solution)/shard_map/ppermute | solution.py:430
  (14 other events, 116.9 us)
